TPU v7x, 32 devices: a whole 2x2x4 slice. The times are simulated.
32 devices in a mesh: px: 4 (over z), py: 8 (over y, x, core).
Axes of the slice: x: 2, y: 2, z: 4, core: 2. Of those that a mesh axis runs over, the one named last changes fastest.
Arguments:
- right_side: float32 [16, 8, 16, 128], P(None, 'px', 'py'), may hold values from -6 to 6
- colour: int32 [8, 16, 128], P('px', 'py'), may hold values from 0 to 3
- active: int32 [8, 16, 128], P('px', 'py'), may hold values 0 or 1
- stress: float32 [6, 8, 16, 128], P(None, 'px', 'py'), may hold values from -1 to 1
- conduct: float32 [8, 16, 128], P('px', 'py'), may hold values from 0.15 to 1.5
- mass: float32 [8, 16, 128], P('px', 'py'), may hold values from 0.25 to 1
- tangent_base: float32 [16, 16], replicated, may hold values from -0.25 to 0.25
- tangent_slope: float32 [6, 16, 16], replicated, may hold values from -0.04 to 0.04
Outputs:
- solution: float32 [16, 8, 16, 128], P(None, 'px', 'py')
All inputs are finite; a program needn't handle non-finite values. No bound on the sum of `active` on one device may be relied on, other than what follows from the above.
Results may differ from a plain program's by a relative error of at most 0.0001.
Values sent between devices are 32-bit elements; how exact they have to be, the bound alone decides.
A program may use at most 64 MiB of HBM per device.

v0:
```python
import jax
import jax.numpy as jnp
from jax import lax
from jax.sharding import PartitionSpec as P

SWEEPS = 2
COLOURS = 4


SHIFT_DIAG = 0.25


def shifted(value, axis, steps):
    count = lax.axis_size(axis)
    first, last = (max(0, -steps), min(count, count - steps))
    return lax.ppermute(value, axis, [(source, source + steps) for source in range(first, last)])


def coupling_table():
    stiff_one = ((1.0, -1.0), (-1.0, 1.0))
    mass_one = ((1.0 / 3.0, 1.0 / 6.0), (1.0 / 6.0, 1.0 / 3.0))
    table = []
    for first in range(8):
        row_values = []
        bits_first = (first >> 2 & 1, first >> 1 & 1, first & 1)
        for second in range(8):
            bits_second = (second >> 2 & 1, second >> 1 & 1, second & 1)
            entry = 0.0
            for direction in range(3):
                term = stiff_one[bits_first[direction]][bits_second[direction]]
                for other in range(3):
                    if other != direction:
                        term = term * mass_one[bits_first[other]][bits_second[other]]
                entry = entry + term
            row_values.append(entry)
        table.append(row_values)
    return table


def corner_bits(corner):
    return (corner >> 2 & 1, corner >> 1 & 1, corner & 1)


def element_tangents(stress, tangent_base, tangent_slope):
    blocks = tangent_base.shape[0]
    identity_block = jnp.eye(blocks, dtype=jnp.float32)[:, :, None, None, None]
    varied = jnp.einsum("kpq,kxyz->pqxyz", tangent_slope, stress, precision=lax.Precision.HIGHEST)
    return identity_block + 0.125 * (tangent_base[:, :, None, None, None] + varied)


def assemble_diag(tangent, diag_weight):
    span_first, span_second, span_third = tangent.shape[2:]
    weighted = tangent * diag_weight[None, None]
    total = jnp.zeros(
        tangent.shape[:2] + (span_first + 1, span_second + 1, span_third + 1), jnp.float32
    )
    for corner in range(8):
        bit_x, bit_y, bit_z = corner_bits(corner)
        total = total.at[
            :,
            :,
            bit_x : bit_x + span_first,
            bit_y : bit_y + span_second,
            bit_z : bit_z + span_third,
        ].add(weighted)
    return total


def apply_elements(tangent, stiff_weight, mass_weight, values):
    span_first, span_second, span_third = tangent.shape[2:]
    corners = []
    for corner in range(8):
        bit_x, bit_y, bit_z = corner_bits(corner)
        corners.append(
            values[
                :,
                bit_x : bit_x + span_first,
                bit_y : bit_y + span_second,
                bit_z : bit_z + span_third,
            ]
        )
    stacked = jnp.stack(corners, axis=1)
    products = jnp.einsum("pqxyz,qbxyz->pbxyz", tangent, stacked, precision=lax.Precision.HIGHEST)
    coupling = jnp.array(coupling_table(), dtype=jnp.float32)
    coupled = jnp.einsum("ab,pbxyz->paxyz", coupling, products, precision=lax.Precision.HIGHEST)
    element_terms = stiff_weight[None, None] * coupled + mass_weight[None, None] * products
    total = jnp.zeros(values.shape, jnp.float32)
    for corner in range(8):
        bit_x, bit_y, bit_z = corner_bits(corner)
        total = total.at[
            :, bit_x : bit_x + span_first, bit_y : bit_y + span_second, bit_z : bit_z + span_third
        ].add(element_terms[:, corner])
    return total


def invert_blocks(matrices):
    order_count = matrices.shape[0]
    working = matrices
    inverse = jnp.broadcast_to(jnp.eye(order_count, dtype=jnp.float32)[:, :, None], matrices.shape)
    for pivot_index in range(order_count):
        pivots = working[pivot_index, pivot_index]
        row_working = working[pivot_index] / pivots[None]
        row_inverse = inverse[pivot_index] / pivots[None]
        factor = working[:, pivot_index]
        working = working - factor[:, None, :] * row_working[None]
        inverse = inverse - factor[:, None, :] * row_inverse[None]
        working = working.at[pivot_index].set(row_working)
        inverse = inverse.at[pivot_index].set(row_inverse)
    return inverse


def fold_diag(total, span_first, span_second, span_third):
    moved = shifted(total[:, :, span_first:, :, :span_third], "px", 1)
    owned = total[:, :, :span_first, :, :span_third]
    owned = owned.at[:, :, 0:1].add(moved)
    moved = shifted(owned[:, :, :, span_second:], "py", 1)
    owned = owned[:, :, :, :span_second]
    return owned.at[:, :, :, 0:1].add(moved)


def fold_partial(total, span_first, span_second, span_third):
    moved = shifted(total[:, span_first:, :, :span_third], "px", 1)
    owned = total[:, :span_first, :, :span_third]
    owned = owned.at[:, 0:1].add(moved)
    moved = shifted(owned[:, :, span_second:], "py", 1)
    owned = owned[:, :, :span_second]
    return owned.at[:, :, 0:1].add(moved)


def fetch_values(field):
    above = shifted(field[:, 0:1], "px", -1)
    wider = jnp.concatenate([field, above], axis=1)
    above = shifted(wider[:, :, 0:1], "py", -1)
    return jnp.concatenate([wider, above], axis=2)


def on_device(right_side, colour, active, stress, conduct, mass, tangent_base, tangent_slope):
    blocks, span_first, span_second, span_third = right_side.shape
    total_first = span_first * lax.axis_size("px")
    total_second = span_second * lax.axis_size("py")
    grid_shape = (span_first, span_second, span_third)
    first_ids = lax.broadcasted_iota(jnp.int32, grid_shape, 0) + lax.axis_index("px") * span_first
    second_ids = lax.broadcasted_iota(jnp.int32, grid_shape, 1) + lax.axis_index("py") * span_second
    third_ids = lax.broadcasted_iota(jnp.int32, grid_shape, 2)
    inside = (
        (first_ids < total_first - 1)
        & (second_ids < total_second - 1)
        & (third_ids < span_third - 1)
    )
    weight = active.astype(jnp.float32) * inside.astype(jnp.float32)
    diag_factor = coupling_table()[0][0]
    tangent = element_tangents(stress, tangent_base, tangent_slope)
    stiff_weight = weight * conduct
    mass_weight = weight * mass * 0.125
    diag_total = assemble_diag(tangent, stiff_weight * diag_factor + mass_weight)
    diag_total = fold_diag(diag_total, span_first, span_second, span_third)
    full = diag_total + SHIFT_DIAG * jnp.eye(blocks, dtype=jnp.float32)[:, :, None, None, None]
    inverse = invert_blocks(full.reshape(blocks, blocks, -1)).reshape(full.shape)
    solution = jnp.zeros(right_side.shape, jnp.float32)
    for sweep_index in range(SWEEPS):
        for colour_index in range(COLOURS):
            near = jnp.pad(fetch_values(solution), ((0, 0), (0, 0), (0, 0), (0, 1)))
            total = apply_elements(tangent, stiff_weight, mass_weight, near)
            resid = right_side - (
                SHIFT_DIAG * solution + fold_partial(total, span_first, span_second, span_third)
            )
            update = jnp.einsum("pqxyz,qxyz->pxyz", inverse, resid, precision=lax.Precision.HIGHEST)
            solution = jnp.where(colour[None] == colour_index, solution + update, solution)
    return solution


def solution(mesh):
    return jax.shard_map(
        on_device,
        mesh=mesh,
        in_specs=(
            P(None, "px", "py", None),
            P("px", "py", None),
            P("px", "py", None),
            P(None, "px", "py", None),
            P("px", "py", None),
            P("px", "py", None),
            P(),
            P(),
        ),
        out_specs=P(None, "px", "py", None),
        check_vma=False,
    )
```

profile of v0, /device:TPU:3, one launch (start us, length us, event | category | flops | bytes accessed | tf_op | source)
XLA Modules:
  0.0 704.5 jit_solution(5648149580073813671)
XLA Ops:
  5.7 11.5 %scatter-add.319 = f32[16,16,3,3,129]{4,1,3,2,0:T(8,128)S(1)} dynamic-update-slice(f32[16,16,3,3,129]{4,1,3,2,0:T(8,128)S(1)} %scatter-add.316, f32[16,16,2,2,128]{4,1,3,2,0:T(8,128)} %fusion.6, s32[]{:T(128)} %constant.2812.clone.1, s32[]{:T(128)} %constant.2812.clone.1, s32[]{:T(128)} %constant.2812.clone.1, s32[]{:T(128)} %constant.2812.clone.1, s32[]{:T(128)} %constant.2811.clone.1) | dynamic-update-slice | bytes 1048580 | tf_op jit(solution)/shard_map/scatter-add | solution.py:65
  18.4 11.5 %scatter-add.321 = f32[16,16,3,3,129]{4,1,3,2,0:T(8,128)S(1)} dynamic-update-slice(f32[16,16,3,3,129]{4,1,3,2,0:T(8,128)S(1)} %fusion.9, f32[16,16,2,2,128]{4,1,3,2,0:T(8,128)} %slice_add_fusion.4, s32[]{:T(128)} %constant.2812.clone.1, s32[]{:T(128)} %constant.2812.clone.1, s32[]{:T(128)} %constant.2812.clone.1, s32[]{:T(128)} %constant.2811.clone.1, s32[]{:T(128)} %constant.2811.clone.1) | dynamic-update-slice | bytes 1048580 | tf_op jit(solution)/shard_map/scatter-add | solution.py:65
  31.0 11.5 %scatter-add.325 = f32[16,16,3,3,129]{4,1,3,2,0:T(8,128)S(1)} dynamic-update-slice(f32[16,16,3,3,129]{4,1,3,2,0:T(8,128)S(1)} %fusion.8, f32[16,16,2,2,128]{4,1,3,2,0:T(8,128)} %slice_add_fusion.2, s32[]{:T(128)} %constant.2812.clone.1, s32[]{:T(128)} %constant.2812.clone.1, s32[]{:T(128)} %constant.2811.clone.1, s32[]{:T(128)} %constant.2812.clone.1, s32[]{:T(128)} %constant.2811.clone.1) | dynamic-update-slice | bytes 1048580 | tf_op jit(solution)/shard_map/scatter-add | solution.py:65
  43.7 11.5 %scatter-add.329 = f32[16,16,3,3,129]{4,1,3,2,0:T(8,128)S(1)} dynamic-update-slice(f32[16,16,3,3,129]{4,1,3,2,0:T(8,128)S(1)} %fusion.7, f32[16,16,2,2,128]{4,1,3,2,0:T(8,128)} %slice_add_fusion, s32[]{:T(128)} %constant.2812.clone.1, s32[]{:T(128)} %constant.2812.clone.1, s32[]{:T(128)} %constant.2811.clone.1, s32[]{:T(128)} %constant.2811.clone.1, s32[]{:T(128)} %constant.2811.clone.1) | dynamic-update-slice | bytes 1048580 | tf_op jit(solution)/shard_map/scatter-add | solution.py:65
  75.3 6.7 stack.224
  82.0 10.9 %fusion.163 = f32[2,2,128,8,16]{4,3,2,1,0:T(8,128)} fusion(f32[16,8,2,2,128]{0,1,4,3,2:T(8,128)} %stack.224, f32[16,16,2,2,128]{1,0,4,3,2:T(8,128)} %copy.658), kind=kOutput, calls=%fused_computation.557 | convolution fusion | flops 12582912 | bytes 1048576 | tf_op jit(solution)/shard_map/pqxyz,qbxyz->pbxyz/dot_general | solution.py:83
  95.8 9.8 %scatter-add.301 = f32[16,3,3,129]{3,2,1,0:T(4,128)S(1)} dynamic-update-slice(f32[16,3,3,129]{3,2,1,0:T(4,128)S(1)} %scatter-add.300, f32[16,2,2,128]{3,2,1,0:T(2,128)S(1)} %fusion.23, s32[]{:T(128)} %constant.2812.clone.1, s32[]{:T(128)} %constant.2812.clone.1, s32[]{:T(128)} %constant.2812.clone.1, s32[]{:T(128)} %constant.2811.clone.1) | dynamic-update-slice | bytes 65540 | tf_op jit(solution)/shard_map/scatter-add | solution.py:92
  107.0 9.8 %scatter-add.305 = f32[16,3,3,129]{3,2,1,0:T(4,128)S(1)} dynamic-update-slice(f32[16,3,3,129]{3,2,1,0:T(4,128)S(1)} %scatter-add.304, f32[16,2,2,128]{3,2,1,0:T(2,128)S(1)} %slice_add_fusion.26, s32[]{:T(128)} %constant.2812.clone.1, s32[]{:T(128)} %constant.2812.clone.1, s32[]{:T(128)} %constant.2811.clone.1, s32[]{:T(128)} %constant.2811.clone.1) | dynamic-update-slice | bytes 65540 | tf_op jit(solution)/shard_map/scatter-add | solution.py:92
  117.1 9.8 %scatter-add.309 = f32[16,3,3,129]{3,2,1,0:T(4,128)S(1)} dynamic-update-slice(f32[16,3,3,129]{3,2,1,0:T(4,128)S(1)} %fusion.117, f32[16,2,2,128]{3,2,1,0:T(2,128)S(1)} %slice_add_fusion.24, s32[]{:T(128)} %constant.2812.clone.1, s32[]{:T(128)} %constant.2811.clone.1, s32[]{:T(128)} %constant.2812.clone.1, s32[]{:T(128)} %constant.2811.clone.1) | dynamic-update-slice | bytes 65540 | tf_op jit(solution)/shard_map/scatter-add | solution.py:92
  128.3 10.4 %scatter-add.311 = f32[16,3,3,129]{3,2,1,0:T(4,128)S(1)} dynamic-update-slice(f32[16,3,3,129]{3,2,1,0:T(4,128)S(1)} %scatter-add.310, f32[16,2,2,128]{3,2,1,0:T(2,128)S(1)} %slice_add_fusion.22, s32[]{:T(128)} %constant.2812.clone.1, s32[]{:T(128)} %constant.2811.clone.1, s32[]{:T(128)} %constant.2811.clone.1, s32[]{:T(128)} %constant.2811.clone.1) | dynamic-update-slice | bytes 65540 | tf_op jit(solution)/shard_map/scatter-add | solution.py:92
  173.7 9.5 %fusion.164 = f32[2,2,128,8,16]{4,3,2,1,0:T(8,128)} fusion(f32[16,8,2,2,128]{0,1,4,3,2:T(8,128)S(1)} %copy.672, f32[16,16,2,2,128]{1,0,4,3,2:T(8,128)} %copy.658), kind=kOutput, calls=%fused_computation.558 | convolution fusion | flops 12582912 | bytes 1048576 | tf_op jit(solution)/shard_map/pqxyz,qbxyz->pbxyz/dot_general | solution.py:83
  186.3 9.8 %scatter-add.335 = f32[16,3,3,129]{3,2,1,0:T(4,128)S(1)} dynamic-update-slice(f32[16,3,3,129]{3,2,1,0:T(4,128)S(1)} %scatter-add.334, f32[16,2,2,128]{3,2,1,0:T(2,128)S(1)} %fusion.24, s32[]{:T(128)} %constant.2812.clone.1, s32[]{:T(128)} %constant.2812.clone.1, s32[]{:T(128)} %constant.2812.clone.1, s32[]{:T(128)} %constant.2811.clone.1) | dynamic-update-slice | bytes 65540 | tf_op jit(solution)/shard_map/scatter-add | solution.py:92
  197.5 9.8 %scatter-add.339 = f32[16,3,3,129]{3,2,1,0:T(4,128)S(1)} dynamic-update-slice(f32[16,3,3,129]{3,2,1,0:T(4,128)S(1)} %scatter-add.336, f32[16,2,2,128]{3,2,1,0:T(2,128)S(1)} %fusion.113, s32[]{:T(128)} %constant.2812.clone.1, s32[]{:T(128)} %constant.2812.clone.1, s32[]{:T(128)} %constant.2811.clone.1, s32[]{:T(128)} %constant.2811.clone.1) | dynamic-update-slice | bytes 65540 | tf_op jit(solution)/shard_map/scatter-add | solution.py:92
  207.5 9.8 %scatter-add.341 = f32[16,3,3,129]{3,2,1,0:T(4,128)S(1)} dynamic-update-slice(f32[16,3,3,129]{3,2,1,0:T(4,128)S(1)} %fusion.112, f32[16,2,2,128]{3,2,1,0:T(2,128)S(1)} %fusion.110, s32[]{:T(128)} %constant.2812.clone.1, s32[]{:T(128)} %constant.2811.clone.1, s32[]{:T(128)} %constant.2812.clone.1, s32[]{:T(128)} %constant.2811.clone.1) | dynamic-update-slice | bytes 65540 | tf_op jit(solution)/shard_map/scatter-add | solution.py:92
  218.7 9.8 %scatter-add.345 = f32[16,3,3,129]{3,2,1,0:T(4,128)S(1)} dynamic-update-slice(f32[16,3,3,129]{3,2,1,0:T(4,128)S(1)} %scatter-add.344, f32[16,2,2,128]{3,2,1,0:T(2,128)S(1)} %fusion.108, s32[]{:T(128)} %constant.2812.clone.1, s32[]{:T(128)} %constant.2811.clone.1, s32[]{:T(128)} %constant.2811.clone.1, s32[]{:T(128)} %constant.2811.clone.1) | dynamic-update-slice | bytes 65540 | tf_op jit(solution)/shard_map/scatter-add | solution.py:92
  251.3 9.6 %fusion.165 = f32[2,2,128,8,16]{4,3,2,1,0:T(8,128)} fusion(f32[16,8,2,2,128]{0,1,4,3,2:T(8,128)S(1)} %copy.677, f32[16,16,2,2,128]{1,0,4,3,2:T(8,128)} %copy.658), kind=kOutput, calls=%fused_computation.559 | convolution fusion | flops 12582912 | bytes 1048576 | tf_op jit(solution)/shard_map/pqxyz,qbxyz->pbxyz/dot_general | solution.py:83
  264.0 9.8 %scatter-add.351 = f32[16,3,3,129]{3,2,1,0:T(4,128)S(1)} dynamic-update-slice(f32[16,3,3,129]{3,2,1,0:T(4,128)S(1)} %scatter-add.350, f32[16,2,2,128]{3,2,1,0:T(2,128)S(1)} %fusion.25, s32[]{:T(128)} %constant.2812.clone.1, s32[]{:T(128)} %constant.2812.clone.1, s32[]{:T(128)} %constant.2812.clone.1, s32[]{:T(128)} %constant.2811.clone.1) | dynamic-update-slice | bytes 65540 | tf_op jit(solution)/shard_map/scatter-add | solution.py:92
  275.2 9.8 %scatter-add.355 = f32[16,3,3,129]{3,2,1,0:T(4,128)S(1)} dynamic-update-slice(f32[16,3,3,129]{3,2,1,0:T(4,128)S(1)} %scatter-add.354, f32[16,2,2,128]{3,2,1,0:T(2,128)S(1)} %fusion.104, s32[]{:T(128)} %constant.2812.clone.1, s32[]{:T(128)} %constant.2812.clone.1, s32[]{:T(128)} %constant.2811.clone.1, s32[]{:T(128)} %constant.2811.clone.1) | dynamic-update-slice | bytes 65540 | tf_op jit(solution)/shard_map/scatter-add | solution.py:92
  285.2 9.8 %scatter-add.359 = f32[16,3,3,129]{3,2,1,0:T(4,128)S(1)} dynamic-update-slice(f32[16,3,3,129]{3,2,1,0:T(4,128)S(1)} %fusion.103, f32[16,2,2,128]{3,2,1,0:T(2,128)S(1)} %fusion.101, s32[]{:T(128)} %constant.2812.clone.1, s32[]{:T(128)} %constant.2811.clone.1, s32[]{:T(128)} %constant.2812.clone.1, s32[]{:T(128)} %constant.2811.clone.1) | dynamic-update-slice | bytes 65540 | tf_op jit(solution)/shard_map/scatter-add | solution.py:92
  296.4 9.8 %scatter-add.361 = f32[16,3,3,129]{3,2,1,0:T(4,128)S(1)} dynamic-update-slice(f32[16,3,3,129]{3,2,1,0:T(4,128)S(1)} %scatter-add.360, f32[16,2,2,128]{3,2,1,0:T(2,128)S(1)} %fusion.99, s32[]{:T(128)} %constant.2812.clone.1, s32[]{:T(128)} %constant.2811.clone.1, s32[]{:T(128)} %constant.2811.clone.1, s32[]{:T(128)} %constant.2811.clone.1) | dynamic-update-slice | bytes 65540 | tf_op jit(solution)/shard_map/scatter-add | solution.py:92
  329.0 9.8 %fusion.166 = f32[2,2,128,8,16]{4,3,2,1,0:T(8,128)} fusion(f32[16,8,2,2,128]{0,1,4,3,2:T(8,128)S(1)} %copy.682, f32[16,16,2,2,128]{1,0,4,3,2:T(8,128)} %copy.658), kind=kOutput, calls=%fused_computation.560 | convolution fusion | flops 12582912 | bytes 1048576 | tf_op jit(solution)/shard_map/pqxyz,qbxyz->pbxyz/dot_general | solution.py:83
  341.8 9.8 %scatter-add.369 = f32[16,3,3,129]{3,2,1,0:T(4,128)S(1)} dynamic-update-slice(f32[16,3,3,129]{3,2,1,0:T(4,128)S(1)} %scatter-add.366, f32[16,2,2,128]{3,2,1,0:T(2,128)S(1)} %fusion.26, s32[]{:T(128)} %constant.2812.clone.1, s32[]{:T(128)} %constant.2812.clone.1, s32[]{:T(128)} %constant.2812.clone.1, s32[]{:T(128)} %constant.2811.clone.1) | dynamic-update-slice | bytes 65540 | tf_op jit(solution)/shard_map/scatter-add | solution.py:92
  353.0 9.8 %scatter-add.371 = f32[16,3,3,129]{3,2,1,0:T(4,128)S(1)} dynamic-update-slice(f32[16,3,3,129]{3,2,1,0:T(4,128)S(1)} %scatter-add.370, f32[16,2,2,128]{3,2,1,0:T(2,128)S(1)} %fusion.95, s32[]{:T(128)} %constant.2812.clone.1, s32[]{:T(128)} %constant.2812.clone.1, s32[]{:T(128)} %constant.2811.clone.1, s32[]{:T(128)} %constant.2811.clone.1) | dynamic-update-slice | bytes 65540 | tf_op jit(solution)/shard_map/scatter-add | solution.py:92
  363.0 9.8 %scatter-add.375 = f32[16,3,3,129]{3,2,1,0:T(4,128)S(1)} dynamic-update-slice(f32[16,3,3,129]{3,2,1,0:T(4,128)S(1)} %fusion.94, f32[16,2,2,128]{3,2,1,0:T(2,128)S(1)} %fusion.92, s32[]{:T(128)} %constant.2812.clone.1, s32[]{:T(128)} %constant.2811.clone.1, s32[]{:T(128)} %constant.2812.clone.1, s32[]{:T(128)} %constant.2811.clone.1) | dynamic-update-slice | bytes 65540 | tf_op jit(solution)/shard_map/scatter-add | solution.py:92
  374.2 9.8 %scatter-add.379 = f32[16,3,3,129]{3,2,1,0:T(4,128)S(1)} dynamic-update-slice(f32[16,3,3,129]{3,2,1,0:T(4,128)S(1)} %scatter-add.376, f32[16,2,2,128]{3,2,1,0:T(2,128)S(1)} %fusion.90, s32[]{:T(128)} %constant.2812.clone.1, s32[]{:T(128)} %constant.2811.clone.1, s32[]{:T(128)} %constant.2811.clone.1, s32[]{:T(128)} %constant.2811.clone.1) | dynamic-update-slice | bytes 65540 | tf_op jit(solution)/shard_map/scatter-add | solution.py:92
  406.8 9.5 %fusion.167 = f32[2,2,128,8,16]{4,3,2,1,0:T(8,128)} fusion(f32[16,8,2,2,128]{0,1,4,3,2:T(8,128)S(1)} %copy.687, f32[16,16,2,2,128]{1,0,4,3,2:T(8,128)} %copy.658), kind=kOutput, calls=%fused_computation.561 | convolution fusion | flops 12582912 | bytes 1048576 | tf_op jit(solution)/shard_map/pqxyz,qbxyz->pbxyz/dot_general | solution.py:83
  419.4 9.8 %scatter-add.385 = f32[16,3,3,129]{3,2,1,0:T(4,128)S(1)} dynamic-update-slice(f32[16,3,3,129]{3,2,1,0:T(4,128)S(1)} %scatter-add.384, f32[16,2,2,128]{3,2,1,0:T(2,128)S(1)} %fusion.27, s32[]{:T(128)} %constant.2812.clone.1, s32[]{:T(128)} %constant.2812.clone.1, s32[]{:T(128)} %constant.2812.clone.1, s32[]{:T(128)} %constant.2811.clone.1) | dynamic-update-slice | bytes 65540 | tf_op jit(solution)/shard_map/scatter-add | solution.py:92
  430.6 9.8 %scatter-add.389 = f32[16,3,3,129]{3,2,1,0:T(4,128)S(1)} dynamic-update-slice(f32[16,3,3,129]{3,2,1,0:T(4,128)S(1)} %scatter-add.386, f32[16,2,2,128]{3,2,1,0:T(2,128)S(1)} %fusion.86, s32[]{:T(128)} %constant.2812.clone.1, s32[]{:T(128)} %constant.2812.clone.1, s32[]{:T(128)} %constant.2811.clone.1, s32[]{:T(128)} %constant.2811.clone.1) | dynamic-update-slice | bytes 65540 | tf_op jit(solution)/shard_map/scatter-add | solution.py:92
  440.6 9.8 %scatter-add.391 = f32[16,3,3,129]{3,2,1,0:T(4,128)S(1)} dynamic-update-slice(f32[16,3,3,129]{3,2,1,0:T(4,128)S(1)} %fusion.85, f32[16,2,2,128]{3,2,1,0:T(2,128)S(1)} %fusion.83, s32[]{:T(128)} %constant.2812.clone.1, s32[]{:T(128)} %constant.2811.clone.1, s32[]{:T(128)} %constant.2812.clone.1, s32[]{:T(128)} %constant.2811.clone.1) | dynamic-update-slice | bytes 65540 | tf_op jit(solution)/shard_map/scatter-add | solution.py:92
  451.8 9.8 %scatter-add.395 = f32[16,3,3,129]{3,2,1,0:T(4,128)S(1)} dynamic-update-slice(f32[16,3,3,129]{3,2,1,0:T(4,128)S(1)} %scatter-add.394, f32[16,2,2,128]{3,2,1,0:T(2,128)S(1)} %fusion.81, s32[]{:T(128)} %constant.2812.clone.1, s32[]{:T(128)} %constant.2811.clone.1, s32[]{:T(128)} %constant.2811.clone.1, s32[]{:T(128)} %constant.2811.clone.1) | dynamic-update-slice | bytes 65540 | tf_op jit(solution)/shard_map/scatter-add | solution.py:92
  477.7 5.4 collective-permute-done.23
  484.4 9.6 %fusion.168 = f32[2,2,128,8,16]{4,3,2,1,0:T(8,128)} fusion(f32[16,8,2,2,128]{0,1,4,3,2:T(8,128)S(1)} %copy.692, f32[16,16,2,2,128]{1,0,4,3,2:T(8,128)} %copy.658), kind=kOutput, calls=%fused_computation.562 | convolution fusion | flops 12582912 | bytes 1048576 | tf_op jit(solution)/shard_map/pqxyz,qbxyz->pbxyz/dot_general | solution.py:83
  497.0 9.8 %scatter-add.401 = f32[16,3,3,129]{3,2,1,0:T(4,128)S(1)} dynamic-update-slice(f32[16,3,3,129]{3,2,1,0:T(4,128)S(1)} %scatter-add.400, f32[16,2,2,128]{3,2,1,0:T(2,128)S(1)} %fusion.28, s32[]{:T(128)} %constant.2812.clone.1, s32[]{:T(128)} %constant.2812.clone.1, s32[]{:T(128)} %constant.2812.clone.1, s32[]{:T(128)} %constant.2811.clone.1) | dynamic-update-slice | bytes 65540 | tf_op jit(solution)/shard_map/scatter-add | solution.py:92
  508.3 9.8 %scatter-add.405 = f32[16,3,3,129]{3,2,1,0:T(4,128)S(1)} dynamic-update-slice(f32[16,3,3,129]{3,2,1,0:T(4,128)S(1)} %scatter-add.404, f32[16,2,2,128]{3,2,1,0:T(2,128)S(1)} %fusion.77, s32[]{:T(128)} %constant.2812.clone.1, s32[]{:T(128)} %constant.2812.clone.1, s32[]{:T(128)} %constant.2811.clone.1, s32[]{:T(128)} %constant.2811.clone.1) | dynamic-update-slice | bytes 65540 | tf_op jit(solution)/shard_map/scatter-add | solution.py:92
  518.3 9.8 %scatter-add.409 = f32[16,3,3,129]{3,2,1,0:T(4,128)S(1)} dynamic-update-slice(f32[16,3,3,129]{3,2,1,0:T(4,128)S(1)} %fusion.76, f32[16,2,2,128]{3,2,1,0:T(2,128)S(1)} %fusion.74, s32[]{:T(128)} %constant.2812.clone.1, s32[]{:T(128)} %constant.2811.clone.1, s32[]{:T(128)} %constant.2812.clone.1, s32[]{:T(128)} %constant.2811.clone.1) | dynamic-update-slice | bytes 65540 | tf_op jit(solution)/shard_map/scatter-add | solution.py:92
  529.5 9.8 %scatter-add.411 = f32[16,3,3,129]{3,2,1,0:T(4,128)S(1)} dynamic-update-slice(f32[16,3,3,129]{3,2,1,0:T(4,128)S(1)} %scatter-add.410, f32[16,2,2,128]{3,2,1,0:T(2,128)S(1)} %fusion.72, s32[]{:T(128)} %constant.2812.clone.1, s32[]{:T(128)} %constant.2811.clone.1, s32[]{:T(128)} %constant.2811.clone.1, s32[]{:T(128)} %constant.2811.clone.1) | dynamic-update-slice | bytes 65540 | tf_op jit(solution)/shard_map/scatter-add | solution.py:92
  555.3 5.4 collective-permute-done.27
  562.0 9.8 %fusion.169 = f32[2,2,128,8,16]{4,3,2,1,0:T(8,128)} fusion(f32[16,8,2,2,128]{0,1,4,3,2:T(8,128)S(1)} %copy.697, f32[16,16,2,2,128]{1,0,4,3,2:T(8,128)} %copy.658), kind=kOutput, calls=%fused_computation.563 | convolution fusion | flops 12582912 | bytes 1048576 | tf_op jit(solution)/shard_map/pqxyz,qbxyz->pbxyz/dot_general | solution.py:83
  574.9 9.8 %scatter-add.419 = f32[16,3,3,129]{3,2,1,0:T(4,128)S(1)} dynamic-update-slice(f32[16,3,3,129]{3,2,1,0:T(4,128)S(1)} %scatter-add.416, f32[16,2,2,128]{3,2,1,0:T(2,128)S(1)} %fusion.29, s32[]{:T(128)} %constant.2812.clone.1, s32[]{:T(128)} %constant.2812.clone.1, s32[]{:T(128)} %constant.2812.clone.1, s32[]{:T(128)} %constant.2811.clone.1) | dynamic-update-slice | bytes 65540 | tf_op jit(solution)/shard_map/scatter-add | solution.py:92
  586.1 9.8 %scatter-add.421 = f32[16,3,3,129]{3,2,1,0:T(4,128)S(1)} dynamic-update-slice(f32[16,3,3,129]{3,2,1,0:T(4,128)S(1)} %scatter-add.420, f32[16,2,2,128]{3,2,1,0:T(2,128)S(1)} %fusion.68, s32[]{:T(128)} %constant.2812.clone.1, s32[]{:T(128)} %constant.2812.clone.1, s32[]{:T(128)} %constant.2811.clone.1, s32[]{:T(128)} %constant.2811.clone.1) | dynamic-update-slice | bytes 65540 | tf_op jit(solution)/shard_map/scatter-add | solution.py:92
  596.1 9.8 %scatter-add.425 = f32[16,3,3,129]{3,2,1,0:T(4,128)S(1)} dynamic-update-slice(f32[16,3,3,129]{3,2,1,0:T(4,128)S(1)} %fusion.67, f32[16,2,2,128]{3,2,1,0:T(2,128)S(1)} %fusion.65, s32[]{:T(128)} %constant.2812.clone.1, s32[]{:T(128)} %constant.2811.clone.1, s32[]{:T(128)} %constant.2812.clone.1, s32[]{:T(128)} %constant.2811.clone.1) | dynamic-update-slice | bytes 65540 | tf_op jit(solution)/shard_map/scatter-add | solution.py:92
  607.3 9.8 %scatter-add.429 = f32[16,3,3,129]{3,2,1,0:T(4,128)S(1)} dynamic-update-slice(f32[16,3,3,129]{3,2,1,0:T(4,128)S(1)} %scatter-add.426, f32[16,2,2,128]{3,2,1,0:T(2,128)S(1)} %fusion.63, s32[]{:T(128)} %constant.2812.clone.1, s32[]{:T(128)} %constant.2811.clone.1, s32[]{:T(128)} %constant.2811.clone.1, s32[]{:T(128)} %constant.2811.clone.1) | dynamic-update-slice | bytes 65540 | tf_op jit(solution)/shard_map/scatter-add | solution.py:92
  633.1 5.4 collective-permute-done.31
  639.9 9.5 %fusion.170 = f32[2,2,128,8,16]{4,3,2,1,0:T(8,128)} fusion(f32[16,8,2,2,128]{0,1,4,3,2:T(8,128)S(1)} %copy.702, f32[16,16,2,2,128]{1,0,4,3,2:T(8,128)} %copy.658), kind=kOutput, calls=%fused_computation.564 | convolution fusion | flops 12582912 | bytes 1048576 | tf_op jit(solution)/shard_map/pqxyz,qbxyz->pbxyz/dot_general | solution.py:83
  652.6 9.8 %scatter-add.435 = f32[16,3,3,129]{3,2,1,0:T(4,128)S(1)} dynamic-update-slice(f32[16,3,3,129]{3,2,1,0:T(4,128)S(1)} %scatter-add.434, f32[16,2,2,128]{3,2,1,0:T(2,128)S(1)} %fusion.30, s32[]{:T(128)} %constant.2812.clone.1, s32[]{:T(128)} %constant.2812.clone.1, s32[]{:T(128)} %constant.2812.clone.1, s32[]{:T(128)} %constant.2811.clone.1) | dynamic-update-slice | bytes 65540 | tf_op jit(solution)/shard_map/scatter-add | solution.py:92
  663.9 9.8 %scatter-add.439 = f32[16,3,3,129]{3,2,1,0:T(4,128)S(1)} dynamic-update-slice(f32[16,3,3,129]{3,2,1,0:T(4,128)S(1)} %scatter-add.436, f32[16,2,2,128]{3,2,1,0:T(2,128)S(1)} %slice_add_fusion.13, s32[]{:T(128)} %constant.2812.clone.1, s32[]{:T(128)} %constant.2812.clone.1, s32[]{:T(128)} %constant.2811.clone.1, s32[]{:T(128)} %constant.2811.clone.1) | dynamic-update-slice | bytes 65540 | tf_op jit(solution)/shard_map/scatter-add | solution.py:92
  673.9 9.8 %scatter-add.441 = f32[16,3,3,129]{3,2,1,0:T(4,128)S(1)} dynamic-update-slice(f32[16,3,3,129]{3,2,1,0:T(4,128)S(1)} %fusion.60, f32[16,2,2,128]{3,2,1,0:T(2,128)S(1)} %slice_add_fusion.11, s32[]{:T(128)} %constant.2812.clone.1, s32[]{:T(128)} %constant.2811.clone.1, s32[]{:T(128)} %constant.2812.clone.1, s32[]{:T(128)} %constant.2811.clone.1) | dynamic-update-slice | bytes 65540 | tf_op jit(solution)/shard_map/scatter-add | solution.py:92
  685.1 9.8 %scatter-add.445 = f32[16,3,3,129]{3,2,1,0:T(4,128)S(1)} dynamic-update-slice(f32[16,3,3,129]{3,2,1,0:T(4,128)S(1)} %scatter-add.444, f32[16,2,2,128]{3,2,1,0:T(2,128)S(1)} %slice_add_fusion.9, s32[]{:T(128)} %constant.2812.clone.1, s32[]{:T(128)} %constant.2811.clone.1, s32[]{:T(128)} %constant.2811.clone.1, s32[]{:T(128)} %constant.2811.clone.1) | dynamic-update-slice | bytes 65540 | tf_op jit(solution)/shard_map/scatter-add | solution.py:92
  (485 shorter events, 238.5 us)
Async XLA Ops:
  0.7 64.7 %collective-permute-start = (f32[16,1,2,128]{0,3,2,1:T(8,128)}, f32[16,1,2,128]{0,3,2,1:T(8,128)S(1)}, u32[]{:S(2)}, u32[]{:S(2)}) collective-permute-start(f32[16,1,2,128]{0,3,2,1:T(8,128)} %slice.4530), channel_id=1, source_target_pairs={{8,0},{16,8},{24,16},{9,1},{17,9},{25,17},{10,2},{18,10},{26,18},{... | collective-permute-start | bytes 49160 | tf_op jit(solution)/shard_map/ppermute | solution.py:16
  56.0 88.9 %collective-permute-start.4 = (f32[16,16,1,3,128]{4,1,3,2,0:T(8,128)}, f32[16,16,1,3,128]{4,1,3,2,0:T(8,128)}, u32[]{:S(2)}, u32[]{:S(2)}) collective-permute-start(f32[16,16,1,3,128]{4,1,3,2,0:T(8,128)} %slice.4878), channel_id=1, source_target_pairs={{0,8},{8,16},{16,24},{1,9},{9,17},{17,25},{2,10},{10,18},{18,26},{... | collective-permute-start | bytes 1179656 | tf_op jit(solution)/shard_map/ppermute | solution.py:16
  65.4 7.9 %collective-permute-start.1 = (f32[16,3,1,128]{0,3,2,1:T(8,128)S(1)}, f32[16,3,1,128]{0,3,2,1:T(8,128)S(1)}, u32[]{:S(2)}, u32[]{:S(2)}) collective-permute-start(f32[16,3,1,128]{0,3,2,1:T(8,128)S(1)} %pad_slice_fusion.38), channel_id=1, source_target_pairs={{1,0},{2,1},{3,2},{4,3},{5,4},{6,5},{7,6},{9,8},{10,9},{11,10},{12... | collective-permute-start | bytes 73736 | tf_op jit(solution)/shard_map/ppermute | solution.py:16
  92.9 2.3 copy-start.2
  117.0 32.5 %copy-start.1 = (f32[16,2,2,128]{3,2,1,0:T(2,128)S(1)}, f32[16,2,2,128]{3,2,1,0:T(2,128)}, u32[]{:S(2)}) copy-start(f32[16,2,2,128]{3,2,1,0:T(2,128)} %param.258) | copy-start | bytes 98308
  138.7 3.5 collective-permute-start.2
  141.2 12.4 %copy-start.4 = (f32[16,16]{1,0:T(8,128)S(1)}, f32[16,16]{1,0:T(8,128)}, u32[]{:S(2)}) copy-start(f32[16,16]{1,0:T(8,128)} %fusion.158) | copy-start | bytes 3076
  142.2 7.2 %collective-permute-start.3 = (f32[16,2,1,128]{3,2,1,0:T(1,128)S(1)}, f32[16,2,1,128]{3,2,1,0:T(1,128)S(1)}, u32[]{:S(2)}, u32[]{:S(2)}) collective-permute-start(f32[16,2,1,128]{3,2,1,0:T(1,128)S(1)} %slice.4869), channel_id=1, source_target_pairs={{0,1},{1,2},{2,3},{3,4},{4,5},{5,6},{6,7},{8,9},{9,10},{10,11},{11... | collective-permute-start | bytes 49160 | tf_op jit(solution)/shard_map/ppermute | solution.py:16
  145.9 0.9 copy-start
  146.8 5.8 collective-permute-start.5
  159.1 0.8 copy-start.3
  159.9 4.8 collective-permute-start.6
  164.7 7.7 %collective-permute-start.7 = (f32[16,3,1,128]{3,2,1,0:T(1,128)S(1)}, f32[16,3,1,128]{3,2,1,0:T(1,128)S(1)}, u32[]{:S(2)}, u32[]{:S(2)}) collective-permute-start(f32[16,3,1,128]{3,2,1,0:T(1,128)S(1)} %fusion.125), channel_id=1, source_target_pairs={{1,0},{2,1},{3,2},{4,3},{5,4},{6,5},{7,6},{9,8},{10,9},{11,10},{12... | collective-permute-start | bytes 73736 | tf_op jit(solution)/shard_map/ppermute | solution.py:16
  185.4 51.9 %copy-start.7 = (pred[2,2,128]{2,1,0:T(4,128)(4,1)S(1)}, pred[2,2,128]{2,1,0:T(4,128)(4,1)}, u32[]{:S(2)}) copy-start(pred[2,2,128]{2,1,0:T(4,128)(4,1)} %get-tuple-element.1527) | copy-start | bytes 1540
  228.6 4.7 collective-permute-start.8
  233.3 3.6 collective-permute-start.9
  237.4 5.1 collective-permute-start.10
  242.5 7.5 %collective-permute-start.11 = (f32[16,3,1,128]{3,2,1,0:T(1,128)S(1)}, f32[16,3,1,128]{3,2,1,0:T(1,128)S(1)}, u32[]{:S(2)}, u32[]{:S(2)}) collective-permute-start(f32[16,3,1,128]{3,2,1,0:T(1,128)S(1)} %fusion.124), channel_id=1, source_target_pairs={{1,0},{2,1},{3,2},{4,3},{5,4},{6,5},{7,6},{9,8},{10,9},{11,10},{12... | collective-permute-start | bytes 73736 | tf_op jit(solution)/shard_map/ppermute | solution.py:16
  263.1 51.9 %copy-start.6 = (pred[2,2,128]{2,1,0:T(4,128)(4,1)S(1)}, pred[2,2,128]{2,1,0:T(4,128)(4,1)}, u32[]{:S(2)}) copy-start(pred[2,2,128]{2,1,0:T(4,128)(4,1)} %get-tuple-element.1525) | copy-start | bytes 1540
  306.3 4.7 collective-permute-start.12
  311.0 3.6 collective-permute-start.13
  315.0 5.3 collective-permute-start.14
  320.4 7.3 %collective-permute-start.15 = (f32[16,3,1,128]{3,2,1,0:T(1,128)S(1)}, f32[16,3,1,128]{3,2,1,0:T(1,128)S(1)}, u32[]{:S(2)}, u32[]{:S(2)}) collective-permute-start(f32[16,3,1,128]{3,2,1,0:T(1,128)S(1)} %fusion.123), channel_id=1, source_target_pairs={{1,0},{2,1},{3,2},{4,3},{5,4},{6,5},{7,6},{9,8},{10,9},{11,10},{12... | collective-permute-start | bytes 73736 | tf_op jit(solution)/shard_map/ppermute | solution.py:16
  340.9 51.9 %copy-start.5 = (pred[2,2,128]{2,1,0:T(4,128)(4,1)S(1)}, pred[2,2,128]{2,1,0:T(4,128)(4,1)}, u32[]{:S(2)}) copy-start(pred[2,2,128]{2,1,0:T(4,128)(4,1)} %get-tuple-element.1524) | copy-start | bytes 1540
  384.1 4.7 collective-permute-start.16
  388.8 3.6 collective-permute-start.17
  392.9 5.1 collective-permute-start.18
  398.0 7.5 %collective-permute-start.19 = (f32[16,3,1,128]{3,2,1,0:T(1,128)S(1)}, f32[16,3,1,128]{3,2,1,0:T(1,128)S(1)}, u32[]{:S(2)}, u32[]{:S(2)}) collective-permute-start(f32[16,3,1,128]{3,2,1,0:T(1,128)S(1)} %fusion.122), channel_id=1, source_target_pairs={{1,0},{2,1},{3,2},{4,3},{5,4},{6,5},{7,6},{9,8},{10,9},{11,10},{12... | collective-permute-start | bytes 73736 | tf_op jit(solution)/shard_map/ppermute | solution.py:16
  461.7 4.7 collective-permute-start.20
  466.4 3.6 collective-permute-start.21
  470.5 5.1 collective-permute-start.22
  475.6 7.5 %collective-permute-start.23 = (f32[16,3,1,128]{3,2,1,0:T(1,128)S(1)}, f32[16,3,1,128]{3,2,1,0:T(1,128)S(1)}, u32[]{:S(2)}, u32[]{:S(2)}) collective-permute-start(f32[16,3,1,128]{3,2,1,0:T(1,128)S(1)} %fusion.121), channel_id=1, source_target_pairs={{1,0},{2,1},{3,2},{4,3},{5,4},{6,5},{7,6},{9,8},{10,9},{11,10},{12... | collective-permute-start | bytes 73736 | tf_op jit(solution)/shard_map/ppermute | solution.py:16
  539.4 4.7 collective-permute-start.24
  544.1 3.6 collective-permute-start.25
  548.1 5.1 collective-permute-start.26
  553.2 7.5 %collective-permute-start.27 = (f32[16,3,1,128]{3,2,1,0:T(1,128)S(1)}, f32[16,3,1,128]{3,2,1,0:T(1,128)S(1)}, u32[]{:S(2)}, u32[]{:S(2)}) collective-permute-start(f32[16,3,1,128]{3,2,1,0:T(1,128)S(1)} %fusion.120), channel_id=1, source_target_pairs={{1,0},{2,1},{3,2},{4,3},{5,4},{6,5},{7,6},{9,8},{10,9},{11,10},{12... | collective-permute-start | bytes 73736 | tf_op jit(solution)/shard_map/ppermute | solution.py:16
  617.2 4.7 collective-permute-start.28
  621.9 3.6 collective-permute-start.29
  625.9 5.1 collective-permute-start.30
  631.0 7.5 %collective-permute-start.31 = (f32[16,3,1,128]{3,2,1,0:T(1,128)S(1)}, f32[16,3,1,128]{3,2,1,0:T(1,128)S(1)}, u32[]{:S(2)}, u32[]{:S(2)}) collective-permute-start(f32[16,3,1,128]{3,2,1,0:T(1,128)S(1)} %fusion.119), channel_id=1, source_target_pairs={{1,0},{2,1},{3,2},{4,3},{5,4},{6,5},{7,6},{9,8},{10,9},{11,10},{12... | collective-permute-start | bytes 73736 | tf_op jit(solution)/shard_map/ppermute | solution.py:16
  694.9 4.7 collective-permute-start.32
  699.6 3.6 collective-permute-start.33
where the time goes:
time: 714 us; the launch traced here: 704 us
  local copies, waits for them, and re-layouts  426 us (60%)
  starting transfers between devices  89.2 us (12%)
  matrix products  83.6 us (12%)
  waiting for transfers between devices  79.5 us (11%)
  other arithmetic  22.5 us (3%)
    scatter-add x56, local copies, waits for them, and re-layouts, apply_elements(): total = total.at[:, bit_x:bit_x + span_first, bit_y:bit_y + span_second,...  335 us
    ppermute x34, starting transfers between devices, shifted(): lax.ppermute(value, axis, [(source, source + steps) for source in range(f...  89.2 us
    ppermute x34, waiting for transfers between devices, shifted(): lax.ppermute(value, axis, [(source, source + steps) for source in range(f...  79.5 us
    dot_general x8, matrix products, apply_elements(): jnp.einsum('pqxyz,qbxyz->pbxyz', tangent, stacked, precision=lax.Precisio...  78.1 us
    scatter-add x5, local copies, waits for them, and re-layouts, assemble_diag(): total = total.at[:, :, bit_x:bit_x + span_first, bit_y:bit_y + span_secon...  46.2 us
    dot_general x8, local copies, waits for them, and re-layouts, apply_elements(): jnp.einsum('pqxyz,qbxyz->pbxyz', tangent, stacked, precision=lax.Precisio...  17.9 us
  transfers between devices with their start and end apart: 34, of which 31 were waited for; matrix products, arithmetic and copies ran while one was open for 18% of the time, Pallas kernels for 0%

commit v1 on v0

v1 whole, which is shorter than its diff:
```python
import functools

import jax
import jax.numpy as jnp
from jax import lax
from jax.experimental import pallas as pl
from jax.experimental.pallas import tpu as pltpu
from jax.sharding import PartitionSpec as P

SWEEPS = 2
COLOURS = 4
SHIFT_DIAG = 0.25
MESH = pl.DeviceIdType.MESH
WAYS = [(dx, dy) for dx in (-1, 0, 1) for dy in (-1, 0, 1) if (dx, dy) != (0, 0)]


def kernel(
    total_x, total_y, rhs_ref, colour_ref, active_ref, stress_ref, conduct_ref, mass_ref, base_ref, slope_ref,
    out_ref, field, elem, weights, inv, mat, coef, send_sem, recv_sem, elem_send, elem_recv,
):
    count_x, count_y = total_x // 2, total_y // 2
    me_x, me_y = lax.axis_index("px"), lax.axis_index("py")
    lanes = rhs_ref.shape[1]
    blocks = base_ref.shape[0]
    stresses = slope_ref.shape[0]
    parts = stresses + 1

    def exists(dx, dy):
        found = None
        for delta, me, count in ((dx, me_x, count_x), (dy, me_y, count_y)):
            if delta == 0:
                continue
            one = me >= 1 if delta < 0 else me <= count - 2
            found = one if found is None else found & one
        return found

    def there(dx, dy):
        return (me_x + dx, me_y + dy)

    elem[...] = jnp.zeros_like(elem)
    field[...] = jnp.zeros_like(field)
    barrier = pltpu.get_barrier_semaphore()
    for dx, dy in WAYS:
        @pl.when(exists(dx, dy))
        def _():
            pl.semaphore_signal(barrier, inc=1, device_id=there(dx, dy), device_id_type=MESH)

    third = lax.broadcasted_iota(jnp.int32, (1, lanes), 1)
    for i in range(2):
        for j in range(2):
            c = 2 * i + j
            inside = (third < lanes - 1) & (2 * me_x + i < total_x - 1) & (2 * me_y + j < total_y - 1)
            weight = jnp.where(inside, active_ref[c : c + 1, :].astype(jnp.float32), 0.0)
            elem[1 + i, 1 + j, 0:stresses, :] = stress_ref[pl.ds(c, stresses, stride=4), :]
            elem[1 + i, 1 + j, stresses : stresses + 1, :] = weight * conduct_ref[c : c + 1, :]
            elem[1 + i, 1 + j, stresses + 1 : stresses + 2, :] = weight * mass_ref[c : c + 1, :] * 0.125

    span_x = 1 + (me_x >= 1).astype(jnp.int32) + (me_x <= count_x - 2).astype(jnp.int32)
    span_y = 1 + (me_y >= 1).astype(jnp.int32) + (me_y <= count_y - 2).astype(jnp.int32)
    pl.semaphore_wait(barrier, span_x * span_y - 1)

    def elem_copy(way, target):
        dx, dy = way
        src = (2 if dx else pl.ds(1, 2), 2 if dy else pl.ds(1, 2))
        dst = (0 if dx else pl.ds(1, 2), 0 if dy else pl.ds(1, 2))
        n = dx * 2 + dy - 1
        return pltpu.make_async_remote_copy(
            src_ref=elem.at[src[0], src[1]], dst_ref=elem.at[dst[0], dst[1]],
            send_sem=elem_send.at[n], recv_sem=elem_recv.at[n], device_id=target, device_id_type=MESH,
        )

    elem_ways = ((0, 1), (1, 0), (1, 1))
    for way in elem_ways:
        @pl.when(exists(*way))
        def _():
            elem_copy(way, there(*way)).start()

    row = lax.broadcasted_iota(jnp.int32, (blocks, blocks), 0)
    col = lax.broadcasted_iota(jnp.int32, (blocks, blocks), 1)
    identity = jnp.where(row == col, 1.0, 0.0).astype(jnp.float32)
    mat[...] = jnp.zeros_like(mat)
    for s in range(parts):
        block = slope_ref[s] * 0.125 if s < stresses else identity + base_ref[...] * 0.125
        mat[:, s * blocks : (s + 1) * blocks] = block
        for q in range(blocks):
            coef[s, q] = jnp.broadcast_to(block[:, q : q + 1], (blocks, lanes))
    high = mat[...].astype(jnp.bfloat16)
    low = (mat[...] - high.astype(jnp.float32)).astype(jnp.bfloat16)
    left = jnp.concatenate(
        [jnp.concatenate([high, high], axis=1), jnp.concatenate([low, low], axis=1)], axis=0
    )

    for dx, dy in elem_ways:
        @pl.when(exists(-dx, -dy))
        def _():
            elem_copy((dx, dy), there(-dx, -dy)).wait_recv()

    line = lax.broadcasted_iota(jnp.int32, (8, lanes), 0)
    diag = {}
    for ex in range(3):
        for ey in range(3):
            part = elem[ex, ey]
            stiff = part[stresses : stresses + 1]
            mass = part[stresses + 1 : stresses + 2]
            scaled = jnp.where(line == stresses, 1.0, part)
            diag[ex, ey] = scaled * (stiff * (1.0 / 3.0) + mass)
            off = scaled * (stiff * (1.0 / 12.0))
            for z, shown in enumerate((off, pltpu.roll(off, 1, 1))):
                for s in range(parts):
                    weights[ex, ey, z, s] = jnp.broadcast_to(shown[s : s + 1], (8, lanes))

    sublane = lax.broadcasted_iota(jnp.int32, (blocks, lanes), 0)
    for i in range(2):
        for j in range(2):
            c = 2 * i + j
            total = diag[i, j] + diag[i + 1, j] + diag[i, j + 1] + diag[i + 1, j + 1]
            total = total + pltpu.roll(total, 1, 1)
            spread = [jnp.broadcast_to(total[s : s + 1], (blocks, lanes)) for s in range(parts)]
            for q in range(blocks):
                value = jnp.where(sublane == q, SHIFT_DIAG, 0.0)
                for s in range(parts):
                    value = value + coef[s, q] * spread[s]
                inv[c, q] = value

    def invert(c, carry):
        columns = [inv[c, q] for q in range(blocks)]
        for r in range(blocks):
            factor = columns[r]
            scale = 1.0 / jnp.broadcast_to(factor[r : r + 1], (8, lanes))
            scale = jnp.concatenate([scale, scale], axis=0)
            for q in range(blocks):
                if q != r:
                    ratio = jnp.broadcast_to(columns[q][r : r + 1], (blocks, lanes)) * scale
                    columns[q] = jnp.where(sublane == r, ratio, columns[q] - factor * ratio)
            columns[r] = jnp.where(sublane == r, scale, -(factor * scale))
        for q in range(blocks):
            inv[c, q] = columns[q]
        return carry

    lax.fori_loop(0, 4, invert, 0)

    def solve(c, vector):
        sums = [None, None]
        for q in range(blocks):
            term = inv[c, q] * jnp.broadcast_to(vector[q : q + 1], (blocks, lanes))
            sums[q % 2] = term if sums[q % 2] is None else sums[q % 2] + term
        return sums[0] + sums[1]

    def field_copy(slot, way, target):
        n = WAYS.index(way)
        src, dst = [], []
        for delta in way:
            src.append({-1: 1, 0: pl.ds(1, 2), 1: 2}[delta])
            dst.append({-1: 3, 0: pl.ds(1, 2), 1: 0}[delta])
        return pltpu.make_async_remote_copy(
            src_ref=field.at[slot, src[0], src[1]], dst_ref=field.at[slot, dst[0], dst[1]],
            send_sem=send_sem.at[slot, n], recv_sem=recv_sem.at[slot, n], device_id=target, device_id_type=MESH,
        )

    def send(slot):
        for way in WAYS:
            @pl.when(exists(*way))
            def _():
                field_copy(slot, way, there(*way)).start()

    for i in range(2):
        for j in range(2):
            c = 2 * i + j
            first = solve(c, rhs_ref[pl.ds(c, blocks, stride=4), :])
            hit = jnp.broadcast_to(colour_ref[c : c + 1, :], (blocks, lanes)) == 0
            field[0, 1 + i, 1 + j] = jnp.where(hit, first, 0.0)
    send(0)
    for way in elem_ways:
        @pl.when(exists(*way))
        def _():
            elem_copy(way, there(*way)).wait_send()

    steps = SWEEPS * COLOURS
    gap = jnp.zeros((128 - parts * blocks, lanes), jnp.bfloat16)

    def step(t, carry):
        old = lax.rem(t + 1, 2)
        new = lax.rem(t, 2)
        for dx, dy in WAYS:
            @pl.when(exists(-dx, -dy))
            def _():
                field_copy(old, (dx, dy), there(-dx, -dy)).wait_recv()
        shade = lax.rem(t, COLOURS)
        fresh = []
        for i in range(2):
            pair = []
            for j in range(2):
                sums = [None] * parts
                for dx in (-1, 1):
                    for dy in (-1, 1):
                        ex, ey = i + (dx > 0), j + (dy > 0)
                        corner = field[old, 1 + i + dx, 1 + j + dy]
                        cross = corner + field[old, 1 + i + dx, 1 + j] + field[old, 1 + i, 1 + j + dy]
                        for z in range(2):
                            q = corner + pltpu.roll(cross, lanes - 1 if z == 0 else 1, 1)
                            for s in range(parts):
                                w = weights[ex, ey, z, s]
                                term = jnp.concatenate([w, w], axis=0) * q
                                sums[s] = term if sums[s] is None else sums[s] + term
                tops = [x.astype(jnp.bfloat16) for x in sums]
                rest = [(x - y.astype(jnp.float32)).astype(jnp.bfloat16) for x, y in zip(sums, tops)]
                pair.append(jnp.concatenate([*tops, gap, *rest, gap], axis=0))
            made = jnp.dot(left, jnp.concatenate(pair, axis=1), preferred_element_type=jnp.float32)
            made = made[:blocks] + made[blocks:]
            for j in range(2):
                c = 2 * i + j
                vector = rhs_ref[pl.ds(c, blocks, stride=4), :] + made[:, j * lanes : (j + 1) * lanes]
                hit = jnp.broadcast_to(colour_ref[c : c + 1, :], (blocks, lanes)) == shade
                fresh.append(jnp.where(hit, solve(c, vector), field[old, 1 + i, 1 + j]))
        for way in WAYS:
            @pl.when(exists(*way))
            def _():
                field_copy(old, way, there(*way)).wait_send()
        for c in range(4):
            field[new, 1 + c // 2, 1 + c % 2] = fresh[c]
        for way in WAYS:
            @pl.when(exists(*way) & (t < steps - 1))
            def _():
                field_copy(new, way, there(*way)).start()
        return carry

    lax.fori_loop(1, steps, step, 0)
    for c in range(4):
        out_ref[pl.ds(c, blocks, stride=4), :] = field[(steps - 1) % 2, 1 + c // 2, 1 + c % 2]


def on_device(right_side, colour, active, stress, conduct, mass, tangent_base, tangent_slope):
    blocks, span_x, span_y, lanes = right_side.shape
    assert (span_x, span_y) == (2, 2)
    stresses = stress.shape[0]
    parts = stresses + 1
    total_x, total_y = span_x * lax.axis_size("px"), span_y * lax.axis_size("py")
    vmem = pl.BlockSpec(memory_space=pltpu.VMEM)
    flat = pl.pallas_call(
        functools.partial(kernel, total_x, total_y),
        out_shape=jax.ShapeDtypeStruct((blocks * 4, lanes), jnp.float32),
        in_specs=[vmem] * 8,
        out_specs=vmem,
        scratch_shapes=[
            pltpu.VMEM((2, 4, 4, blocks, lanes), jnp.float32),
            pltpu.VMEM((3, 3, stresses + 2, lanes), jnp.float32),
            pltpu.VMEM((3, 3, 2, parts, 8, lanes), jnp.float32),
            pltpu.VMEM((4, blocks, blocks, lanes), jnp.float32),
            pltpu.VMEM((blocks, 128), jnp.float32),
            pltpu.VMEM((parts, blocks, blocks, lanes), jnp.float32),
            pltpu.SemaphoreType.DMA((2, 8)),
            pltpu.SemaphoreType.DMA((2, 8)),
            pltpu.SemaphoreType.DMA((3,)),
            pltpu.SemaphoreType.DMA((3,)),
        ],
        compiler_params=pltpu.CompilerParams(
            collective_id=0, has_side_effects=True, vmem_limit_bytes=24 * 1024 * 1024
        ),
        name="gauss_seidel",
    )(
        right_side.reshape(blocks * 4, lanes),
        colour.reshape(4, lanes),
        active.reshape(4, lanes),
        stress.reshape(stresses * 4, lanes),
        conduct.reshape(4, lanes),
        mass.reshape(4, lanes),
        tangent_base,
        tangent_slope,
    )
    return flat.reshape(right_side.shape)


def solution(mesh):
    return jax.shard_map(
        on_device,
        mesh=mesh,
        in_specs=(
            P(None, "px", "py", None),
            P("px", "py", None),
            P("px", "py", None),
            P(None, "px", "py", None),
            P("px", "py", None),
            P("px", "py", None),
            P(),
            P(),
        ),
        out_specs=P(None, "px", "py", None),
        check_vma=False,
    )
```

time: 714 us -> 40.5 us (0.06); the launches traced: 704 us -> 40.1 us
  local copies, waits for them, and re-layouts: 426 us -> 5.62 us
  starting transfers between devices: 89.2 us -> 0 us
  matrix products: 83.6 us -> 0 us
  waiting for transfers between devices: 79.5 us -> 0 us
  Pallas kernels: 0 us -> 34.5 us
  other arithmetic: 22.5 us -> 0 us
    scatter-add x69 -> x0, local copies, waits for them, and re-layouts: 382 us -> none  [the longest x56 335 us: apply_elements(): total = total.at[:, bit_x:bit_x + span_first, bit_y:bit_y + span_second,...]
    ppermute x34 -> x0, starting transfers between devices: 89.2 us -> none  [shifted(): lax.ppermute(value, axis, [(source, source + steps) for source in range(f...]
    dot_general x17 -> x0, matrix products: 83.6 us -> none  [the longest x8 78.1 us: apply_elements(): jnp.einsum('pqxyz,qbxyz->pbxyz', tangent, stacked, precision=lax.Precisio...]
    ppermute x34 -> x0, waiting for transfers between devices: 79.5 us -> none  [shifted(): lax.ppermute(value, axis, [(source, source + steps) for source in range(f...]
    pallas_call x0 -> x1, Pallas kernels: none -> 34.5 us  [on_device(): pl.pallas_call(functools.partial(kernel, total_x, total_y), out_shape=jax...]
    dot_general x8 -> x0, local copies, waits for them, and re-layouts: 17.9 us -> none  [apply_elements(): jnp.einsum('pqxyz,qbxyz->pbxyz', tangent, stacked, precision=lax.Precisio...]
    another operation x16 -> x0, local copies, waits for them, and re-layouts: 12.7 us -> none  [apply_elements(): stacked = jnp.stack(corners, axis=1)]
    add x68 -> x0, other arithmetic: 9.95 us -> none  [the longest x4 4.14 us: assemble_diag(): total = total.at[:, :, bit_x:bit_x + span_first, bit_y:bit_y + span_secon...]
  transfers between devices with their start and end apart: 34 -> 0, of which waited for: 31 -> 0; matrix products, arithmetic and copies ran while one was open for 18% -> 0% of each run, Pallas kernels for 0% -> 0%
where the time goes in v1:
time: 40.5 us; the launch traced here: 40.1 us
  Pallas kernels  34.5 us (85%)
  local copies, waits for them, and re-layouts  5.62 us (14%)
    pallas_call x1, Pallas kernels, on_device(): pl.pallas_call(functools.partial(kernel, total_x, total_y), out_shape=jax...  34.5 us
    unnamed x17, local copies, waits for them, and re-layouts  5.62 us

profile of v1, /device:TPU:3, one launch (start us, length us, event | category | flops | bytes accessed | tf_op | source)
XLA Modules:
  0.0 40.1 jit_solution(2102624441608128905)
XLA Ops:
  0.0 0.0 copy-start.3
  0.0 0.0 copy-start.4
  0.0 0.7 %copy-done.3 = f32[16,16]{1,0:T(8,128)S(1)} copy-done((f32[16,16]{1,0:T(8,128)S(1)}, f32[16,16]{1,0:T(8,128)}, u32[]{:S(2)}) %copy-start.3) | copy-done | bytes 1048
  0.7 0.0 copy-done.4
  0.7 0.0 copy-start
  0.7 0.8 %copy-done = f32[6,16,16]{2,1,0:T(8,128)S(1)} copy-done((f32[6,16,16]{2,1,0:T(8,128)S(1)}, f32[6,16,16]{2,1,0:T(8,128)}, u32[]{:S(2)}) %copy-start) | copy-done | bytes 6168
  1.5 0.0 copy-start.1
  1.5 0.8 %copy-done.1 = f32[16,2,2,128]{3,2,1,0:T(2,128)S(1)} copy-done((f32[16,2,2,128]{3,2,1,0:T(2,128)S(1)}, f32[16,2,2,128]{3,2,1,0:T(2,128)}, u32[]{:S(2)}) %copy-start.1) | copy-done | bytes 32792
  2.3 0.0 copy-start.2
  2.3 0.7 %copy-done.2 = f32[6,2,2,128]{3,2,1,0:T(2,128)S(1)} copy-done((f32[6,2,2,128]{3,2,1,0:T(2,128)S(1)}, f32[6,2,2,128]{3,2,1,0:T(2,128)}, u32[]{:S(2)}) %copy-start.2) | copy-done | bytes 12312
  3.0 0.0 copy-start.5
  3.0 0.7 %copy-done.5 = s32[2,2,128]{2,1,0:T(2,128)S(1)} copy-done((s32[2,2,128]{2,1,0:T(2,128)S(1)}, s32[2,2,128]{2,1,0:T(2,128)}, u32[]{:S(2)}) %copy-start.5) | copy-done | bytes 2072
  3.6 0.0 copy-start.6
  3.6 0.7 %copy-done.6 = f32[2,2,128]{2,1,0:T(2,128)S(1)} copy-done((f32[2,2,128]{2,1,0:T(2,128)S(1)}, f32[2,2,128]{2,1,0:T(2,128)}, u32[]{:S(2)}) %copy-start.6) | copy-done | bytes 2072
  4.3 0.0 copy-start.7
  4.3 0.7 %copy-done.7 = f32[2,2,128]{2,1,0:T(2,128)S(1)} copy-done((f32[2,2,128]{2,1,0:T(2,128)S(1)}, f32[2,2,128]{2,1,0:T(2,128)}, u32[]{:S(2)}) %copy-start.7) | copy-done | bytes 2072
  5.0 34.5 %gauss_seidel.1 = f32[64,128]{1,0:T(8,128)S(1)} custom-call(f32[64,128]{1,0:T(8,128)S(1)} %bitcast.8, s32[4,128]{1,0:T(4,128)S(1)} %bitcast.10, s32[4,128]{1,0:T(4,128)S(1)} %bitcast.11, f32[24,128]{1,0:T(8,128)S(1)} %bitcast.9, f32[4,128]{1,0:T(4,128)S(1)} %bitcast.12, f32[4,128]{1,0:T(4,128)S(1)} %bitcast.13, f32[16,16]{1,0:T(8,128)S(1)} %copy-done.3, ...), custom_call_target="tpu_custom_call" | custom-call | tf_op jit(solution)/shard_map/gauss_seidel/pallas_call | solution.py:239
  39.5 0.6 %copy.10 = f32[16,2,2,128]{3,2,1,0:T(2,128)} copy(f32[16,2,2,128]{3,2,1,0:T(2,128)S(1)} %bitcast.7) | data formatting | bytes 65536
Async XLA Ops:
  0.0 0.7 %copy-start.3 = (f32[16,16]{1,0:T(8,128)S(1)}, f32[16,16]{1,0:T(8,128)}, u32[]{:S(2)}) copy-start(f32[16,16]{1,0:T(8,128)} %base_ref.1) | copy-start | bytes 3076
  0.0 0.7 %copy-start.4 = (s32[2,2,128]{2,1,0:T(2,128)S(1)}, s32[2,2,128]{2,1,0:T(2,128)}, u32[]{:S(2)}) copy-start(s32[2,2,128]{2,1,0:T(2,128)} %param.9) | copy-start | bytes 6148
  0.7 0.8 %copy-start = (f32[6,16,16]{2,1,0:T(8,128)S(1)}, f32[6,16,16]{2,1,0:T(8,128)}, u32[]{:S(2)}) copy-start(f32[6,16,16]{2,1,0:T(8,128)} %slope_ref.1) | copy-start | bytes 18436
  1.5 0.8 %copy-start.1 = (f32[16,2,2,128]{3,2,1,0:T(2,128)S(1)}, f32[16,2,2,128]{3,2,1,0:T(2,128)}, u32[]{:S(2)}) copy-start(f32[16,2,2,128]{3,2,1,0:T(2,128)} %param.8) | copy-start | bytes 98308
  2.3 0.7 %copy-start.2 = (f32[6,2,2,128]{3,2,1,0:T(2,128)S(1)}, f32[6,2,2,128]{3,2,1,0:T(2,128)}, u32[]{:S(2)}) copy-start(f32[6,2,2,128]{3,2,1,0:T(2,128)} %param.11) | copy-start | bytes 36868
  3.0 0.7 %copy-start.5 = (s32[2,2,128]{2,1,0:T(2,128)S(1)}, s32[2,2,128]{2,1,0:T(2,128)}, u32[]{:S(2)}) copy-start(s32[2,2,128]{2,1,0:T(2,128)} %param.10) | copy-start | bytes 6148
  3.6 0.7 %copy-start.6 = (f32[2,2,128]{2,1,0:T(2,128)S(1)}, f32[2,2,128]{2,1,0:T(2,128)}, u32[]{:S(2)}) copy-start(f32[2,2,128]{2,1,0:T(2,128)} %param.12) | copy-start | bytes 6148
  4.3 0.7 %copy-start.7 = (f32[2,2,128]{2,1,0:T(2,128)S(1)}, f32[2,2,128]{2,1,0:T(2,128)}, u32[]{:S(2)}) copy-start(f32[2,2,128]{2,1,0:T(2,128)} %param.13) | copy-start | bytes 6148

commit v2 on v1

--- a/solution.py
+++ b/solution.py
@@ -15,9 +15,14 @@
 
 
 def kernel(
-    total_x, total_y, rhs_ref, colour_ref, active_ref, stress_ref, conduct_ref, mass_ref, base_ref, slope_ref,
-    out_ref, field, elem, weights, inv, mat, coef, send_sem, recv_sem, elem_send, elem_recv,
+    total_x, total_y, *refs
 ):
+    given, out_ref, staged = refs[:8], refs[8], refs[9:17]
+    rhs_ref, colour_ref, active_ref, stress_ref, conduct_ref, mass_ref, base_ref, slope_ref = staged
+    given_sem, field, elem, weights, inv, mat, coef, send_sem, recv_sem, elem_send, elem_recv = refs[17:]
+    fetches = [pltpu.make_async_copy(a, b, given_sem.at[n]) for n, (a, b) in enumerate(zip(given, staged))]
+    for fetch in fetches:
+        fetch.start()
     count_x, count_y = total_x // 2, total_y // 2
     me_x, me_y = lax.axis_index("px"), lax.axis_index("py")
     lanes = rhs_ref.shape[1]
@@ -44,6 +49,9 @@
         @pl.when(exists(dx, dy))
         def _():
             pl.semaphore_signal(barrier, inc=1, device_id=there(dx, dy), device_id_type=MESH)
+
+    for fetch in fetches:
+        fetch.wait()
 
     third = lax.broadcasted_iota(jnp.int32, (1, lanes), 1)
     for i in range(2):
@@ -236,12 +244,24 @@
     parts = stresses + 1
     total_x, total_y = span_x * lax.axis_size("px"), span_y * lax.axis_size("py")
     vmem = pl.BlockSpec(memory_space=pltpu.VMEM)
+    operands = (
+        right_side.reshape(blocks * 4, lanes),
+        colour.reshape(4, lanes),
+        active.reshape(4, lanes),
+        stress.reshape(stresses * 4, lanes),
+        conduct.reshape(4, lanes),
+        mass.reshape(4, lanes),
+        tangent_base,
+        tangent_slope,
+    )
     flat = pl.pallas_call(
         functools.partial(kernel, total_x, total_y),
         out_shape=jax.ShapeDtypeStruct((blocks * 4, lanes), jnp.float32),
-        in_specs=[vmem] * 8,
+        in_specs=[pl.BlockSpec(memory_space=pltpu.HBM)] * 8,
         out_specs=vmem,
         scratch_shapes=[
+            *[pltpu.VMEM(x.shape, x.dtype) for x in operands],
+            pltpu.SemaphoreType.DMA((8,)),
             pltpu.VMEM((2, 4, 4, blocks, lanes), jnp.float32),
             pltpu.VMEM((3, 3, stresses + 2, lanes), jnp.float32),
             pltpu.VMEM((3, 3, 2, parts, 8, lanes), jnp.float32),
@@ -254,19 +274,10 @@
             pltpu.SemaphoreType.DMA((3,)),
         ],
         compiler_params=pltpu.CompilerParams(
-            collective_id=0, has_side_effects=True, vmem_limit_bytes=24 * 1024 * 1024
+            collective_id=0, has_side_effects=True, vmem_limit_bytes=60 * 1024 * 1024
         ),
         name="gauss_seidel",
-    )(
-        right_side.reshape(blocks * 4, lanes),
-        colour.reshape(4, lanes),
-        active.reshape(4, lanes),
-        stress.reshape(stresses * 4, lanes),
-        conduct.reshape(4, lanes),
-        mass.reshape(4, lanes),
-        tangent_base,
-        tangent_slope,
-    )
+    )(*operands)
     return flat.reshape(right_side.shape)
 
 

time: 40.5 us -> 36.8 us (0.909)
  local copies, waits for them, and re-layouts: 5.62 us -> 1.38 us
  Pallas kernels: 34.5 us -> 35.2 us
    unnamed x17 -> x1, local copies, waits for them, and re-layouts: 5.62 us -> 1.38 us
    pallas_call x1, Pallas kernels: 34.5 us -> 35.2 us  [on_device(): pl.pallas_call(functools.partial(kernel, total_x, total_y), out_shape=jax...]
where the time goes in v2:
time: 36.8 us; the launch traced here: 36.5 us
  Pallas kernels  35.2 us (96%)
  local copies, waits for them, and re-layouts  1.38 us (4%)
    pallas_call x1, Pallas kernels, on_device(): pl.pallas_call(functools.partial(kernel, total_x, total_y), out_shape=jax...  35.2 us
    unnamed x1, local copies, waits for them, and re-layouts  1.38 us

profile of v2, /device:TPU:3, one launch (start us, length us, event | category | flops | bytes accessed | tf_op | source)
XLA Modules:
  0.0 36.5 jit_solution(5942050572953738610)
XLA Ops:
  0.0 35.2 %gauss_seidel.1 = f32[64,128]{1,0:T(8,128)} custom-call(f32[64,128]{1,0:T(8,128)} %bitcast.8, s32[4,128]{1,0:T(4,128)} %bitcast.10, s32[4,128]{1,0:T(4,128)} %bitcast.11, f32[24,128]{1,0:T(8,128)} %bitcast.9, f32[4,128]{1,0:T(4,128)} %bitcast.12, f32[4,128]{1,0:T(4,128)} %bitcast.13, f32[16,16]{1,0:T(8,128)} %refs_6_.1, f32[6,16,16]{2,1,0:T(8,128)} %refs_7_.1), custom_call_target="tpu_custom_call" | custom-call | tf_op jit(solution)/shard_map/gauss_seidel/pallas_call | solution.py:257
  35.2 1.4 %copy.10 = f32[16,2,2,128]{3,2,1,0:T(2,128)} copy(f32[16,2,2,128]{3,2,1,0:T(2,128)} %bitcast.7) | data formatting | bytes 65536

commit v3 on v2

v3 whole, which is shorter than its diff:
```python
import functools

import jax
import jax.numpy as jnp
from jax import lax
from jax.experimental import pallas as pl
from jax.experimental.pallas import tpu as pltpu
from jax.sharding import PartitionSpec as P

SWEEPS = 2
COLOURS = 4
SHIFT_DIAG = 0.25
MESH = pl.DeviceIdType.MESH
WAYS = [(dx, dy) for dx in (-1, 0, 1) for dy in (-1, 0, 1) if (dx, dy) != (0, 0)]


def kernel(total_x, total_y, *refs):
    given, out_ref, staged = refs[:8], refs[8], refs[9:17]
    rhs_ref, colour_ref, active_ref, stress_ref, conduct_ref, mass_ref, base_ref, slope_ref = staged
    given_sem, field, mid, pack, diag, weights, inv, mat, coef, send_sem, recv_sem, pack_send, pack_recv = refs[17:]
    fetches = [pltpu.make_async_copy(a, b, given_sem.at[n]) for n, (a, b) in enumerate(zip(given, staged))]
    for fetch in fetches:
        fetch.start()
    count_x, count_y = total_x // 2, total_y // 2
    me_x, me_y = lax.axis_index("px"), lax.axis_index("py")
    lanes = rhs_ref.shape[1]
    blocks = base_ref.shape[0]
    stresses = slope_ref.shape[0]
    parts = stresses + 1
    pairs = SWEEPS * COLOURS // 2

    def exists(dx, dy):
        found = None
        for delta, me, count in ((dx, me_x, count_x), (dy, me_y, count_y)):
            if delta == 0:
                continue
            one = me >= 1 if delta < 0 else me <= count - 2
            found = one if found is None else found & one
        return found

    def there(dx, dy):
        return (me_x + dx, me_y + dy)

    pack[...] = jnp.zeros_like(pack)
    field[...] = jnp.zeros_like(field)
    barrier = pltpu.get_barrier_semaphore()
    for dx, dy in WAYS:
        @pl.when(exists(dx, dy))
        def _():
            pl.semaphore_signal(barrier, inc=1, device_id=there(dx, dy), device_id_type=MESH)

    for fetch in fetches:
        fetch.wait()

    third = lax.broadcasted_iota(jnp.int32, (1, lanes), 1)
    first_stress, stiff_row = blocks, blocks + stresses
    for i in range(2):
        for j in range(2):
            c = 2 * i + j
            inside = (third < lanes - 1) & (2 * me_x + i < total_x - 1) & (2 * me_y + j < total_y - 1)
            weight = jnp.where(inside, active_ref[c : c + 1, :].astype(jnp.float32), 0.0)
            pack[2 + i, 2 + j, 0:blocks, :] = rhs_ref[pl.ds(c, blocks, stride=4), :]
            pack[2 + i, 2 + j, first_stress:stiff_row, :] = stress_ref[pl.ds(c, stresses, stride=4), :]
            pack[2 + i, 2 + j, stiff_row : stiff_row + 1, :] = weight * conduct_ref[c : c + 1, :]
            pack[2 + i, 2 + j, stiff_row + 1 : stiff_row + 2, :] = weight * mass_ref[c : c + 1, :] * 0.125
            pack[2 + i, 2 + j, stiff_row + 2 : stiff_row + 3, :] = colour_ref[c : c + 1, :].astype(jnp.float32)

    span_x = 1 + (me_x >= 1).astype(jnp.int32) + (me_x <= count_x - 2).astype(jnp.int32)
    span_y = 1 + (me_y >= 1).astype(jnp.int32) + (me_y <= count_y - 2).astype(jnp.int32)
    pl.semaphore_wait(barrier, span_x * span_y - 1)

    def pack_copy(way, target):
        n = WAYS.index(way)
        src = [pl.ds(2, 1) if delta < 0 else pl.ds(2, 2) for delta in way]
        dst = [{-1: pl.ds(4, 1), 0: pl.ds(2, 2), 1: pl.ds(0, 2)}[delta] for delta in way]
        return pltpu.make_async_remote_copy(
            src_ref=pack.at[src[0], src[1]], dst_ref=pack.at[dst[0], dst[1]],
            send_sem=pack_send.at[n], recv_sem=pack_recv.at[n], device_id=target, device_id_type=MESH,
        )

    for way in WAYS:
        @pl.when(exists(*way))
        def _():
            pack_copy(way, there(*way)).start()

    row = lax.broadcasted_iota(jnp.int32, (blocks, blocks), 0)
    col = lax.broadcasted_iota(jnp.int32, (blocks, blocks), 1)
    identity = jnp.where(row == col, 1.0, 0.0).astype(jnp.float32)
    mat[...] = jnp.zeros_like(mat)
    for s in range(parts):
        block = slope_ref[s] * 0.125 if s < stresses else identity + base_ref[...] * 0.125
        mat[:, s * blocks : (s + 1) * blocks] = block
        for q in range(blocks):
            coef[s, q] = jnp.broadcast_to(block[:, q : q + 1], (blocks, lanes))
    high = mat[...].astype(jnp.bfloat16)
    low = (mat[...] - high.astype(jnp.float32)).astype(jnp.bfloat16)
    left = jnp.concatenate(
        [jnp.concatenate([high, high], axis=1), jnp.concatenate([low, low], axis=1)], axis=0
    )

    for dx, dy in WAYS:
        @pl.when(exists(-dx, -dy))
        def _():
            pack_copy((dx, dy), there(-dx, -dy)).wait_recv()

    line = lax.broadcasted_iota(jnp.int32, (8, lanes), 0)

    def weigh(n, carry):
        ex, ey = n // 5, lax.rem(n, 5)
        part = pack[ex, ey, first_stress : first_stress + 8]
        stiff = part[stresses : stresses + 1]
        mass = part[stresses + 1 : stresses + 2]
        scaled = jnp.where(line == stresses, 1.0, part)
        diag[ex, ey] = scaled * (stiff * (1.0 / 3.0) + mass)
        off = scaled * (stiff * (1.0 / 12.0))
        for z, shown in enumerate((off, pltpu.roll(off, 1, 1))):
            for s in range(parts):
                weights[ex, ey, z, s] = jnp.broadcast_to(shown[s : s + 1], (8, lanes))
        return carry

    lax.fori_loop(0, 25, weigh, 0)

    sublane = lax.broadcasted_iota(jnp.int32, (blocks, lanes), 0)

    def matches(a, b, shade):
        shown = pack[a, b, stiff_row + 2 : stiff_row + 3]
        return jnp.broadcast_to(shown, (blocks, lanes)) == shade

    def solve(columns, vector):
        sums = [None, None]
        for q in range(blocks):
            term = columns(q) * jnp.broadcast_to(vector[q : q + 1], (blocks, lanes))
            sums[q % 2] = term if sums[q % 2] is None else sums[q % 2] + term
        return sums[0] + sums[1]

    def invert(n, carry):
        a, b = n // 4, lax.rem(n, 4)
        total = diag[a, b] + diag[a + 1, b] + diag[a, b + 1] + diag[a + 1, b + 1]
        total = total + pltpu.roll(total, 1, 1)
        spread = [jnp.broadcast_to(total[s : s + 1], (blocks, lanes)) for s in range(parts)]
        columns = []
        for q in range(blocks):
            value = jnp.where(sublane == q, SHIFT_DIAG, 0.0)
            for s in range(parts):
                value = value + coef[s, q] * spread[s]
            columns.append(value)
        for r in range(blocks):
            factor = columns[r]
            scale = 1.0 / jnp.broadcast_to(factor[r : r + 1], (8, lanes))
            scale = jnp.concatenate([scale, scale], axis=0)
            for q in range(blocks):
                if q != r:
                    ratio = jnp.broadcast_to(columns[q][r : r + 1], (blocks, lanes)) * scale
                    columns[q] = jnp.where(sublane == r, ratio, columns[q] - factor * ratio)
            columns[r] = jnp.where(sublane == r, scale, -(factor * scale))
        for q in range(blocks):
            inv[a, b, q] = columns[q]
        first = solve(lambda q: columns[q], pack[a + 1, b + 1, 0:blocks])
        mid[a + 1, b + 1] = jnp.where(matches(a + 1, b + 1, 0.0), first, 0.0)
        return carry

    lax.fori_loop(0, 16, invert, 0)

    def field_copy(slot, way, target):
        n = WAYS.index(way)
        dst = [pl.ds({-1: 4, 0: 2, 1: 0}[delta], 2) for delta in way]
        return pltpu.make_async_remote_copy(
            src_ref=field.at[slot, pl.ds(2, 2), pl.ds(2, 2)], dst_ref=field.at[slot, dst[0], dst[1]],
            send_sem=send_sem.at[slot, n], recv_sem=recv_sem.at[slot, n], device_id=target, device_id_type=MESH,
        )

    gap = jnp.zeros((128 - parts * blocks, lanes), jnp.bfloat16)

    def update(read, write, a, places, shade):
        for b0 in places:
            pair = []
            for b in (b0, b0 + 1):
                sums = [None] * parts
                for dx in (-1, 1):
                    for dy in (-1, 1):
                        ex, ey = a if dx > 0 else a - 1, b if dy > 0 else b - 1
                        corner = read(a + dx, b + dy)
                        cross = corner + read(a + dx, b) + read(a, b + dy)
                        for z in range(2):
                            q = corner + pltpu.roll(cross, lanes - 1 if z == 0 else 1, 1)
                            for s in range(parts):
                                w = weights[ex, ey, z, s]
                                term = jnp.concatenate([w, w], axis=0) * q
                                sums[s] = term if sums[s] is None else sums[s] + term
                tops = [x.astype(jnp.bfloat16) for x in sums]
                rest = [(x - y.astype(jnp.float32)).astype(jnp.bfloat16) for x, y in zip(sums, tops)]
                pair.append(jnp.concatenate([*tops, gap, *rest, gap], axis=0))
            made = jnp.dot(left, jnp.concatenate(pair, axis=1), preferred_element_type=jnp.float32)
            made = made[:blocks] + made[blocks:]
            for k in range(2):
                b = b0 + k
                vector = pack[a, b, 0:blocks] + made[:, k * lanes : (k + 1) * lanes]
                value = solve(lambda q: inv[a - 1, b - 1, q], vector)
                write(a, b, jnp.where(matches(a, b, shade), value, read(a, b)))

    def pair_of_steps(p, carry):
        @pl.when(p > 0)
        def _():
            for dx, dy in WAYS:
                @pl.when(exists(-dx, -dy))
                def _():
                    field_copy(p - 1, (dx, dy), there(-dx, -dy)).wait_recv()

            def wide(a, inner):
                def write(x, y, value):
                    mid[x, y] = value

                shade = lax.rem(2 * p, COLOURS).astype(jnp.float32)
                update(lambda x, y: field[p - 1, x, y], write, a, (1, 3), shade)
                return inner

            lax.fori_loop(1, 5, wide, 0)

        def write(x, y, value):
            field[p, x, y] = value

        shade = lax.rem(2 * p + 1, COLOURS).astype(jnp.float32)
        for a in (2, 3):
            update(lambda x, y: mid[x, y], write, a, (2,), shade)
        for way in WAYS:
            @pl.when(exists(*way) & (p < pairs - 1))
            def _():
                field_copy(p, way, there(*way)).start()
        return carry

    lax.fori_loop(0, pairs, pair_of_steps, 0)
    for c in range(4):
        out_ref[pl.ds(c, blocks, stride=4), :] = field[pairs - 1, 2 + c // 2, 2 + c % 2]
    for way in WAYS:
        @pl.when(exists(*way))
        def _():
            pack_copy(way, there(*way)).wait_send()
            for p in range(pairs - 1):
                field_copy(p, way, there(*way)).wait_send()


def on_device(right_side, colour, active, stress, conduct, mass, tangent_base, tangent_slope):
    blocks, span_x, span_y, lanes = right_side.shape
    assert (span_x, span_y) == (2, 2)
    stresses = stress.shape[0]
    parts = stresses + 1
    pairs = SWEEPS * COLOURS // 2
    total_x, total_y = span_x * lax.axis_size("px"), span_y * lax.axis_size("py")
    vmem = pl.BlockSpec(memory_space=pltpu.VMEM)
    operands = (
        right_side.reshape(blocks * 4, lanes),
        colour.reshape(4, lanes),
        active.reshape(4, lanes),
        stress.reshape(stresses * 4, lanes),
        conduct.reshape(4, lanes),
        mass.reshape(4, lanes),
        tangent_base,
        tangent_slope,
    )
    flat = pl.pallas_call(
        functools.partial(kernel, total_x, total_y),
        out_shape=jax.ShapeDtypeStruct((blocks * 4, lanes), jnp.float32),
        in_specs=[pl.BlockSpec(memory_space=pltpu.HBM)] * 8,
        out_specs=vmem,
        scratch_shapes=[
            *[pltpu.VMEM(x.shape, x.dtype) for x in operands],
            pltpu.SemaphoreType.DMA((8,)),
            pltpu.VMEM((pairs, 6, 6, blocks, lanes), jnp.float32),
            pltpu.VMEM((6, 6, blocks, lanes), jnp.float32),
            pltpu.VMEM((6, 6, 32, lanes), jnp.float32),
            pltpu.VMEM((5, 5, 8, lanes), jnp.float32),
            pltpu.VMEM((5, 5, 2, parts, 8, lanes), jnp.float32),
            pltpu.VMEM((4, 4, blocks, blocks, lanes), jnp.float32),
            pltpu.VMEM((blocks, 128), jnp.float32),
            pltpu.VMEM((parts, blocks, blocks, lanes), jnp.float32),
            pltpu.SemaphoreType.DMA((pairs - 1, 8)),
            pltpu.SemaphoreType.DMA((pairs - 1, 8)),
            pltpu.SemaphoreType.DMA((8,)),
            pltpu.SemaphoreType.DMA((8,)),
        ],
        compiler_params=pltpu.CompilerParams(
            collective_id=0, has_side_effects=True, vmem_limit_bytes=60 * 1024 * 1024
        ),
        name="gauss_seidel",
    )(*operands)
    return flat.reshape(right_side.shape)


def solution(mesh):
    return jax.shard_map(
        on_device,
        mesh=mesh,
        in_specs=(
            P(None, "px", "py", None),
            P("px", "py", None),
            P("px", "py", None),
            P(None, "px", "py", None),
            P("px", "py", None),
            P("px", "py", None),
            P(),
            P(),
        ),
        out_specs=P(None, "px", "py", None),
        check_vma=False,
    )
```

time: 36.8 us -> 39.9 us (1.084)
  Pallas kernels: 35.2 us -> 38.2 us
    pallas_call x1, Pallas kernels: 35.2 us -> 38.2 us  [on_device(): pl.pallas_call(functools.partial(kernel, total_x, total_y), out_shape=jax...]
where the time goes in v3:
time: 39.9 us; the launch traced here: 39.6 us
  Pallas kernels  38.2 us (96%)
  local copies, waits for them, and re-layouts  1.38 us (3%)
    pallas_call x1, Pallas kernels, on_device(): pl.pallas_call(functools.partial(kernel, total_x, total_y), out_shape=jax...  38.2 us
    unnamed x1, local copies, waits for them, and re-layouts  1.38 us

profile of v3, /device:TPU:3, one launch (start us, length us, event | category | flops | bytes accessed | tf_op | source)
XLA Modules:
  0.0 39.6 jit_solution(9665716067709799796)
XLA Ops:
  0.0 38.2 %gauss_seidel.1 = f32[64,128]{1,0:T(8,128)} custom-call(f32[64,128]{1,0:T(8,128)} %bitcast.8, s32[4,128]{1,0:T(4,128)} %bitcast.10, s32[4,128]{1,0:T(4,128)} %bitcast.11, f32[24,128]{1,0:T(8,128)} %bitcast.9, f32[4,128]{1,0:T(4,128)} %bitcast.12, f32[4,128]{1,0:T(4,128)} %bitcast.13, f32[16,16]{1,0:T(8,128)} %refs_6_.1, f32[6,16,16]{2,1,0:T(8,128)} %refs_7_.1), custom_call_target="tpu_custom_call" | custom-call | tf_op jit(solution)/shard_map/gauss_seidel/pallas_call | solution.py:260
  38.2 1.4 %copy.10 = f32[16,2,2,128]{3,2,1,0:T(2,128)} copy(f32[16,2,2,128]{3,2,1,0:T(2,128)} %bitcast.7) | data formatting | bytes 65536

commit v4 on v2

--- a/solution.py
+++ b/solution.py
@@ -11,7 +11,9 @@
 COLOURS = 4
 SHIFT_DIAG = 0.25
 MESH = pl.DeviceIdType.MESH
-WAYS = [(dx, dy) for dx in (-1, 0, 1) for dy in (-1, 0, 1) if (dx, dy) != (0, 0)]
+SIDES = [(-1, 0), (1, 0), (0, -1), (0, 1)]
+CORNERS = [(-1, -1), (-1, 1), (1, -1), (1, 1)]
+WAYS = CORNERS + SIDES
 
 
 def kernel(
@@ -187,20 +189,23 @@
     gap = jnp.zeros((128 - parts * blocks, lanes), jnp.bfloat16)
 
     def step(t, carry):
-        old = lax.rem(t + 1, 2)
-        new = lax.rem(t, 2)
-        for dx, dy in WAYS:
-            @pl.when(exists(-dx, -dy))
-            def _():
-                field_copy(old, (dx, dy), there(-dx, -dy)).wait_recv()
+        old, new = t - 1, t
         shade = lax.rem(t, COLOURS)
-        fresh = []
-        for i in range(2):
-            pair = []
-            for j in range(2):
-                sums = [None] * parts
+        sums = [[None] * parts for _ in range(4)]
+
+        def receive(ways):
+            for dx, dy in ways:
+                @pl.when(exists(-dx, -dy))
+                def _():
+                    field_copy(old, (dx, dy), there(-dx, -dy)).wait_recv()
+
+        def gather(outward):
+            for c in range(4):
+                i, j = c // 2, c % 2
                 for dx in (-1, 1):
                     for dy in (-1, 1):
+                        if (dx != 1 - 2 * i) + (dy != 1 - 2 * j) != outward:
+                            continue
                         ex, ey = i + (dx > 0), j + (dy > 0)
                         corner = field[old, 1 + i + dx, 1 + j + dy]
                         cross = corner + field[old, 1 + i + dx, 1 + j] + field[old, 1 + i, 1 + j + dy]
@@ -209,9 +214,19 @@
                             for s in range(parts):
                                 w = weights[ex, ey, z, s]
                                 term = jnp.concatenate([w, w], axis=0) * q
-                                sums[s] = term if sums[s] is None else sums[s] + term
-                tops = [x.astype(jnp.bfloat16) for x in sums]
-                rest = [(x - y.astype(jnp.float32)).astype(jnp.bfloat16) for x, y in zip(sums, tops)]
+                                sums[c][s] = term if sums[c][s] is None else sums[c][s] + term
+
+        gather(0)
+        receive(SIDES)
+        gather(1)
+        receive(CORNERS)
+        gather(2)
+        fresh = []
+        for i in range(2):
+            pair = []
+            for j in range(2):
+                tops = [x.astype(jnp.bfloat16) for x in sums[2 * i + j]]
+                rest = [(x - y.astype(jnp.float32)).astype(jnp.bfloat16) for x, y in zip(sums[2 * i + j], tops)]
                 pair.append(jnp.concatenate([*tops, gap, *rest, gap], axis=0))
             made = jnp.dot(left, jnp.concatenate(pair, axis=1), preferred_element_type=jnp.float32)
             made = made[:blocks] + made[blocks:]
@@ -220,10 +235,6 @@
                 vector = rhs_ref[pl.ds(c, blocks, stride=4), :] + made[:, j * lanes : (j + 1) * lanes]
                 hit = jnp.broadcast_to(colour_ref[c : c + 1, :], (blocks, lanes)) == shade
                 fresh.append(jnp.where(hit, solve(c, vector), field[old, 1 + i, 1 + j]))
-        for way in WAYS:
-            @pl.when(exists(*way))
-            def _():
-                field_copy(old, way, there(*way)).wait_send()
         for c in range(4):
             field[new, 1 + c // 2, 1 + c % 2] = fresh[c]
         for way in WAYS:
@@ -234,7 +245,16 @@
 
     lax.fori_loop(1, steps, step, 0)
     for c in range(4):
-        out_ref[pl.ds(c, blocks, stride=4), :] = field[(steps - 1) % 2, 1 + c // 2, 1 + c % 2]
+        out_ref[pl.ds(c, blocks, stride=4), :] = field[steps - 1, 1 + c // 2, 1 + c % 2]
+
+    def finish(t, carry):
+        for way in WAYS:
+            @pl.when(exists(*way))
+            def _():
+                field_copy(t, way, there(*way)).wait_send()
+        return carry
+
+    lax.fori_loop(0, steps - 1, finish, 0)
 
 
 def on_device(right_side, colour, active, stress, conduct, mass, tangent_base, tangent_slope):
@@ -242,6 +262,7 @@
     assert (span_x, span_y) == (2, 2)
     stresses = stress.shape[0]
     parts = stresses + 1
+    steps = SWEEPS * COLOURS
     total_x, total_y = span_x * lax.axis_size("px"), span_y * lax.axis_size("py")
     vmem = pl.BlockSpec(memory_space=pltpu.VMEM)
     operands = (
@@ -262,14 +283,14 @@
         scratch_shapes=[
             *[pltpu.VMEM(x.shape, x.dtype) for x in operands],
             pltpu.SemaphoreType.DMA((8,)),
-            pltpu.VMEM((2, 4, 4, blocks, lanes), jnp.float32),
+            pltpu.VMEM((steps, 4, 4, blocks, lanes), jnp.float32),
             pltpu.VMEM((3, 3, stresses + 2, lanes), jnp.float32),
             pltpu.VMEM((3, 3, 2, parts, 8, lanes), jnp.float32),
             pltpu.VMEM((4, blocks, blocks, lanes), jnp.float32),
             pltpu.VMEM((blocks, 128), jnp.float32),
             pltpu.VMEM((parts, blocks, blocks, lanes), jnp.float32),
-            pltpu.SemaphoreType.DMA((2, 8)),
-            pltpu.SemaphoreType.DMA((2, 8)),
+            pltpu.SemaphoreType.DMA((steps - 1, 8)),
+            pltpu.SemaphoreType.DMA((steps - 1, 8)),
             pltpu.SemaphoreType.DMA((3,)),
             pltpu.SemaphoreType.DMA((3,)),
         ],

time: 36.8 us -> 36.3 us (0.986)
  Pallas kernels: 35.2 us -> 34.6 us
    pallas_call x1, Pallas kernels: 35.2 us -> 34.6 us  [on_device(): pl.pallas_call(functools.partial(kernel, total_x, total_y), out_shape=jax...]
where the time goes in v4:
time: 36.3 us; the launch traced here: 36 us
  Pallas kernels  34.6 us (95%)
  local copies, waits for them, and re-layouts  1.38 us (4%)
    pallas_call x1, Pallas kernels, on_device(): pl.pallas_call(functools.partial(kernel, total_x, total_y), out_shape=jax...  34.6 us
    unnamed x1, local copies, waits for them, and re-layouts  1.38 us

profile of v4, /device:TPU:3, one launch (start us, length us, event | category | flops | bytes accessed | tf_op | source)
XLA Modules:
  0.0 36.0 jit_solution(16177302181162447265)
XLA Ops:
  0.0 34.6 %gauss_seidel.1 = f32[64,128]{1,0:T(8,128)} custom-call(f32[64,128]{1,0:T(8,128)} %bitcast.8, s32[4,128]{1,0:T(4,128)} %bitcast.10, s32[4,128]{1,0:T(4,128)} %bitcast.11, f32[24,128]{1,0:T(8,128)} %bitcast.9, f32[4,128]{1,0:T(4,128)} %bitcast.12, f32[4,128]{1,0:T(4,128)} %bitcast.13, f32[16,16]{1,0:T(8,128)} %refs_6_.1, f32[6,16,16]{2,1,0:T(8,128)} %refs_7_.1), custom_call_target="tpu_custom_call" | custom-call | tf_op jit(solution)/shard_map/gauss_seidel/pallas_call | solution.py:278
  34.7 1.4 %copy.10 = f32[16,2,2,128]{3,2,1,0:T(2,128)} copy(f32[16,2,2,128]{3,2,1,0:T(2,128)} %bitcast.7) | data formatting | bytes 65536

commit v5 on v4

--- a/solution.py
+++ b/solution.py
@@ -80,7 +80,7 @@
         )
 
     elem_ways = ((0, 1), (1, 0), (1, 1))
-    for way in elem_ways:
+    for way in elem_ways[::-1]:
         @pl.when(exists(*way))
         def _():
             elem_copy(way, there(*way)).start()
@@ -100,37 +100,38 @@
         [jnp.concatenate([high, high], axis=1), jnp.concatenate([low, low], axis=1)], axis=0
     )
 
-    for dx, dy in elem_ways:
+    line = lax.broadcasted_iota(jnp.int32, (8, lanes), 0)
+    diag = {}
+
+    def weigh(ex, ey):
+        part = elem[ex, ey]
+        stiff = part[stresses : stresses + 1]
+        mass = part[stresses + 1 : stresses + 2]
+        scaled = jnp.where(line == stresses, 1.0, part)
+        diag[ex, ey] = scaled * (stiff * (1.0 / 3.0) + mass)
+        off = scaled * (stiff * (1.0 / 12.0))
+        for z, shown in enumerate((off, pltpu.roll(off, 1, 1))):
+            for s in range(parts):
+                weights[ex, ey, z, s] = jnp.broadcast_to(shown[s : s + 1], (8, lanes))
+
+    sublane = lax.broadcasted_iota(jnp.int32, (blocks, lanes), 0)
+
+    def assemble(i, j):
+        total = diag[i, j] + diag[i + 1, j] + diag[i, j + 1] + diag[i + 1, j + 1]
+        total = total + pltpu.roll(total, 1, 1)
+        spread = [jnp.broadcast_to(total[s : s + 1], (blocks, lanes)) for s in range(parts)]
+        for q in range(blocks):
+            value = jnp.where(sublane == q, SHIFT_DIAG, 0.0)
+            for s in range(parts):
+                value = value + coef[s, q] * spread[s]
+            inv[2 * i + j, q] = value
+
+    def receive_elem(way):
+        dx, dy = way
+
         @pl.when(exists(-dx, -dy))
         def _():
-            elem_copy((dx, dy), there(-dx, -dy)).wait_recv()
-
-    line = lax.broadcasted_iota(jnp.int32, (8, lanes), 0)
-    diag = {}
-    for ex in range(3):
-        for ey in range(3):
-            part = elem[ex, ey]
-            stiff = part[stresses : stresses + 1]
-            mass = part[stresses + 1 : stresses + 2]
-            scaled = jnp.where(line == stresses, 1.0, part)
-            diag[ex, ey] = scaled * (stiff * (1.0 / 3.0) + mass)
-            off = scaled * (stiff * (1.0 / 12.0))
-            for z, shown in enumerate((off, pltpu.roll(off, 1, 1))):
-                for s in range(parts):
-                    weights[ex, ey, z, s] = jnp.broadcast_to(shown[s : s + 1], (8, lanes))
-
-    sublane = lax.broadcasted_iota(jnp.int32, (blocks, lanes), 0)
-    for i in range(2):
-        for j in range(2):
-            c = 2 * i + j
-            total = diag[i, j] + diag[i + 1, j] + diag[i, j + 1] + diag[i + 1, j + 1]
-            total = total + pltpu.roll(total, 1, 1)
-            spread = [jnp.broadcast_to(total[s : s + 1], (blocks, lanes)) for s in range(parts)]
-            for q in range(blocks):
-                value = jnp.where(sublane == q, SHIFT_DIAG, 0.0)
-                for s in range(parts):
-                    value = value + coef[s, q] * spread[s]
-                inv[c, q] = value
+            elem_copy(way, there(-dx, -dy)).wait_recv()
 
     def invert(c, carry):
         columns = [inv[c, q] for q in range(blocks)]
@@ -147,7 +148,24 @@
             inv[c, q] = columns[q]
         return carry
 
-    lax.fori_loop(0, 4, invert, 0)
+    for ex in (1, 2):
+        for ey in (1, 2):
+            weigh(ex, ey)
+    assemble(1, 1)
+    lax.fori_loop(3, 4, invert, 0)
+    receive_elem((0, 1))
+    weigh(1, 0)
+    weigh(2, 0)
+    assemble(1, 0)
+    receive_elem((1, 0))
+    weigh(0, 1)
+    weigh(0, 2)
+    assemble(0, 1)
+    lax.fori_loop(1, 3, invert, 0)
+    receive_elem((1, 1))
+    weigh(0, 0)
+    assemble(0, 0)
+    lax.fori_loop(0, 1, invert, 0)
 
     def solve(c, vector):
         sums = [None, None]

time: 36.3 us -> 35.5 us (0.978)
  Pallas kernels: 34.6 us -> 33.9 us
    pallas_call x1, Pallas kernels: 34.6 us -> 33.9 us  [on_device(): pl.pallas_call(functools.partial(kernel, total_x, total_y), out_shape=jax...]
where the time goes in v5:
time: 35.5 us; the launch traced here: 35.3 us
  Pallas kernels  33.9 us (95%)
  local copies, waits for them, and re-layouts  1.38 us (4%)
    pallas_call x1, Pallas kernels, on_device(): pl.pallas_call(functools.partial(kernel, total_x, total_y), out_shape=jax...  33.9 us
    unnamed x1, local copies, waits for them, and re-layouts  1.38 us

profile of v5, /device:TPU:3, one launch (start us, length us, event | category | flops | bytes accessed | tf_op | source)
XLA Modules:
  0.0 35.3 jit_solution(13336951059235193028)
XLA Ops:
  0.0 33.9 %gauss_seidel.1 = f32[64,128]{1,0:T(8,128)} custom-call(f32[64,128]{1,0:T(8,128)} %bitcast.8, s32[4,128]{1,0:T(4,128)} %bitcast.10, s32[4,128]{1,0:T(4,128)} %bitcast.11, f32[24,128]{1,0:T(8,128)} %bitcast.9, f32[4,128]{1,0:T(4,128)} %bitcast.12, f32[4,128]{1,0:T(4,128)} %bitcast.13, f32[16,16]{1,0:T(8,128)} %refs_6_.1, f32[6,16,16]{2,1,0:T(8,128)} %refs_7_.1), custom_call_target="tpu_custom_call" | custom-call | tf_op jit(solution)/shard_map/gauss_seidel/pallas_call | solution.py:296
  33.9 1.4 %copy.10 = f32[16,2,2,128]{3,2,1,0:T(2,128)} copy(f32[16,2,2,128]{3,2,1,0:T(2,128)} %bitcast.7) | data formatting | bytes 65536

commit v6 on v5

--- a/solution.py
+++ b/solution.py
@@ -239,7 +239,6 @@
         gather(1)
         receive(CORNERS)
         gather(2)
-        fresh = []
         for i in range(2):
             pair = []
             for j in range(2):
@@ -252,13 +251,14 @@
                 c = 2 * i + j
                 vector = rhs_ref[pl.ds(c, blocks, stride=4), :] + made[:, j * lanes : (j + 1) * lanes]
                 hit = jnp.broadcast_to(colour_ref[c : c + 1, :], (blocks, lanes)) == shade
-                fresh.append(jnp.where(hit, solve(c, vector), field[old, 1 + i, 1 + j]))
-        for c in range(4):
-            field[new, 1 + c // 2, 1 + c % 2] = fresh[c]
-        for way in WAYS:
-            @pl.when(exists(*way) & (t < steps - 1))
-            def _():
-                field_copy(new, way, there(*way)).start()
+                field[new, 1 + i, 1 + j] = jnp.where(hit, solve(c, vector), field[old, 1 + i, 1 + j])
+            for way in WAYS:
+                if (way[0] == -1) != (i == 0):
+                    continue
+
+                @pl.when(exists(*way) & (t < steps - 1))
+                def _():
+                    field_copy(new, way, there(*way)).start()
         return carry
 
     lax.fori_loop(1, steps, step, 0)

time: 35.5 us -> 35.4 us (level)
  no operation moved by 1% of the time
where the time goes in v6:
time: 35.4 us; the launch traced here: 35.1 us
  Pallas kernels  33.7 us (95%)
  local copies, waits for them, and re-layouts  1.38 us (4%)
    pallas_call x1, Pallas kernels, on_device(): pl.pallas_call(functools.partial(kernel, total_x, total_y), out_shape=jax...  33.7 us
    unnamed x1, local copies, waits for them, and re-layouts  1.38 us

profile of v6, /device:TPU:3, one launch (start us, length us, event | category | flops | bytes accessed | tf_op | source)
XLA Modules:
  0.0 35.1 jit_solution(13330812052468615160)
XLA Ops:
  0.0 33.7 %gauss_seidel.1 = f32[64,128]{1,0:T(8,128)} custom-call(f32[64,128]{1,0:T(8,128)} %bitcast.8, s32[4,128]{1,0:T(4,128)} %bitcast.10, s32[4,128]{1,0:T(4,128)} %bitcast.11, f32[24,128]{1,0:T(8,128)} %bitcast.9, f32[4,128]{1,0:T(4,128)} %bitcast.12, f32[4,128]{1,0:T(4,128)} %bitcast.13, f32[16,16]{1,0:T(8,128)} %refs_6_.1, f32[6,16,16]{2,1,0:T(8,128)} %refs_7_.1), custom_call_target="tpu_custom_call" | custom-call | tf_op jit(solution)/shard_map/gauss_seidel/pallas_call | solution.py:296
  33.7 1.4 %copy.10 = f32[16,2,2,128]{3,2,1,0:T(2,128)} copy(f32[16,2,2,128]{3,2,1,0:T(2,128)} %bitcast.7) | data formatting | bytes 65536
